TPU v7x, 32 devices: a whole 2x2x4 slice. The times are simulated.
32 devices in a mesh: pipe: 2 (over x), dp: 2 (over y), tensor: 8 (over z, core).
Axes of the slice: x: 2, y: 2, z: 4, core: 2. Of those that a mesh axis runs over, the one named last changes fastest.
Arguments:
- layer_input: bfloat16 [4, 2, 1024, 1024], P(None, 'dp', 'tensor'), may hold values from -6 to 6
- segment_ids: int32 [4, 2, 1024], P(None, 'dp'), may hold values from 0 to 7, as said below
- out_cotangent: bfloat16 [4, 2, 1024, 1024], P(None, 'dp', 'tensor'), may hold values from -6 to 6
- norm_gain: float32 [2, 1024], P('pipe'), may hold values from 0.5 to 1.5
- w_zx: bfloat16 [2, 2, 1024, 2048], P('pipe', None, None, 'tensor'), may hold values from -0.1875 to 0.1875
- w_bc: bfloat16 [2, 1024, 256], P('pipe', None, 'tensor'), may hold values from -0.1875 to 0.1875
- w_dt: bfloat16 [2, 1024, 32], P('pipe', None, 'tensor'), may hold values from -0.1875 to 0.1875
- conv_x: float32 [2, 4, 2048], P('pipe', None, 'tensor'), may hold values from -0.5 to 0.5
- conv_x_bias: float32 [2, 2048], P('pipe', 'tensor'), may hold values from -0.5 to 0.5
- conv_bc: float32 [2, 4, 256], P('pipe', None, 'tensor'), may hold values from -0.5 to 0.5
- conv_bc_bias: float32 [2, 256], P('pipe', 'tensor'), may hold values from -0.5 to 0.5
- dt_bias: float32 [2, 32], P('pipe', 'tensor'), may hold values from -6 to -2
- a_log: float32 [2, 32], P('pipe', 'tensor'), may hold values from 0 to 2.77
- d_skip: float32 [2, 32], P('pipe', 'tensor'), may hold values from 0.1 to 1.9
- gate_gain: bfloat16 [2, 2048], P('pipe', 'tensor'), may hold values from 0.5 to 1.5
- w_out: bfloat16 [2, 2048, 1024], P('pipe', 'tensor'), may hold values from -0.125 to 0.125
Outputs:
- layer_outputs: bfloat16 [2, 4, 2, 1024, 1024], P('pipe', None, 'dp', 'tensor')
- input_grads: bfloat16 [2, 4, 2, 1024, 1024], P('pipe', None, 'dp', 'tensor')
- grad_norm_gain: float32 [2, 1024], P('pipe')
- grad_w_zx: float32 [2, 2, 1024, 2048], P('pipe', None, None, 'tensor')
- grad_w_bc: float32 [2, 1024, 256], P('pipe', None, 'tensor')
- grad_w_dt: float32 [2, 1024, 32], P('pipe', None, 'tensor')
- grad_conv_x: float32 [2, 4, 2048], P('pipe', None, 'tensor')
- grad_conv_x_bias: float32 [2, 2048], P('pipe', 'tensor')
- grad_conv_bc: float32 [2, 4, 256], P('pipe', None, 'tensor')
- grad_conv_bc_bias: float32 [2, 256], P('pipe', 'tensor')
- grad_dt_bias: float32 [2, 32], P('pipe', 'tensor')
- grad_a_log: float32 [2, 32], P('pipe', 'tensor')
- grad_d_skip: float32 [2, 32], P('pipe', 'tensor')
- grad_gate_gain: float32 [2, 2048], P('pipe', 'tensor')
- grad_w_out: float32 [2, 2048, 1024], P('pipe', 'tensor')
Inputs may be any that keep to these rules, and one draw needn't show every extreme that they name: `segment_ids`: within each sequence the ids start at 0 and never fall; equal ids form one document. For each index of the second dimension one micro-batch, drawn from the seed, holds a single document over the whole sequence, and another reaches the largest id.
All inputs are finite; a program needn't handle non-finite values.
Results may differ from a plain program's by a relative error of at most 0.025.
Values may be sent and summed in bfloat16 or wider, within the bound.
A program may use at most 192 MiB of HBM per device.

v0:
```python
import jax
import jax.numpy as jnp
from jax import lax
from jax.sharding import PartitionSpec as P

INNER = 2048
BLOCK = 256


EPSILON = 1e-05
PRECISE = lax.Precision.HIGHEST


def shifted(value, axis, steps):
    count = lax.axis_size(axis)
    first, last = (max(0, -steps), min(count, count - steps))
    return lax.ppermute(value, axis, [(source, source + steps) for source in range(first, last)])


def causal_conv(values, kernel, offset_bias, segments):
    taps_count = kernel.shape[0]
    length = values.shape[0]
    padded = jnp.pad(values, ((taps_count - 1, 0), (0, 0)))
    padded_ids = jnp.pad(segments, (taps_count - 1, 0), constant_values=-1)
    result = jnp.zeros_like(values) + offset_bias
    for offset in range(taps_count):
        first_row = taps_count - 1 - offset
        earlier = padded[first_row : first_row + length]
        same_doc = (padded_ids[first_row : first_row + length] == segments).astype(values.dtype)
        result = result + kernel[offset] * earlier * same_doc[:, None]
    return result


def state_scan(inputs, step_sizes, decay_rates, b_values, c_values, segments, block_size):
    length, head_count, head_width = inputs.shape
    blocks = length // block_size
    state_count = b_values.shape[1]
    log_decay = (step_sizes * decay_rates).reshape(blocks, block_size, head_count)
    cumul = jnp.cumsum(log_decay, axis=1)
    weighted = (inputs * step_sizes[:, :, None]).reshape(blocks, block_size, head_count, head_width)
    b_blocks = b_values.reshape(blocks, block_size, state_count)
    c_blocks = c_values.reshape(blocks, block_size, state_count)
    block_ids = segments.reshape(blocks, block_size)
    lower_mask = jnp.tril(jnp.ones((block_size, block_size), inputs.dtype))
    same_doc = (block_ids[:, :, None] == block_ids[:, None, :]).astype(inputs.dtype) * lower_mask
    cumul_heads = jnp.transpose(cumul, (0, 2, 1))
    log_gaps = cumul_heads[:, :, :, None] - cumul_heads[:, :, None, :]
    mask_heads = same_doc[:, None]
    decays = jnp.exp(jnp.where(mask_heads > 0, log_gaps, 0.0)) * mask_heads
    affinity = jnp.einsum("ctn,csn->cts", c_blocks, b_blocks, precision=PRECISE)
    inside = jnp.einsum("chts,cshp->cthp", affinity[:, None] * decays, weighted, precision=PRECISE)
    ending = cumul[:, -1, :]
    to_end = (
        jnp.exp(ending[:, None, :] - cumul)
        * (block_ids == block_ids[:, -1:]).astype(inputs.dtype)[:, :, None]
    )
    block_states = jnp.einsum(
        "csn,cshp->chnp", b_blocks, weighted * to_end[:, :, :, None], precision=PRECISE
    )
    before = jnp.concatenate([jnp.full((1,), -1, jnp.int32), block_ids[:-1, -1]])
    carry_keep = jnp.exp(ending) * (block_ids[:, -1] == before).astype(inputs.dtype)[:, None]
    running = jnp.zeros_like(block_states[0])
    entering = []
    for block_index in range(blocks):
        entering.append(running)
        running = carry_keep[block_index][:, None, None] * running + block_states[block_index]
    entering = jnp.stack(entering)
    from_start = jnp.exp(cumul) * (block_ids == before[:, None]).astype(inputs.dtype)[:, :, None]
    across = (
        jnp.einsum("ctn,chnp->cthp", c_blocks, entering, precision=PRECISE)
        * from_start[:, :, :, None]
    )
    return (inside + across).reshape(length, head_count, head_width)


def mixer(
    x_proj,
    step_raw,
    bc_values,
    gate_raw,
    kernel_x,
    offset_x,
    step_bias,
    decay_log,
    skip_gain,
    segments,
    block_size,
):
    mixed_in = jax.nn.silu(causal_conv(x_proj, kernel_x, offset_x, segments))
    length = x_proj.shape[0]
    head_count = step_raw.shape[1]
    step_sizes = jax.nn.softplus(step_raw + step_bias)
    decay_rates = -jnp.exp(decay_log)
    state_count = bc_values.shape[1] // 2
    per_head = mixed_in.reshape(length, head_count, -1)
    scanned = state_scan(
        per_head,
        step_sizes,
        decay_rates,
        bc_values[:, :state_count],
        bc_values[:, state_count:],
        segments,
        block_size,
    )
    outputs = (scanned + skip_gain[None, :, None] * per_head).reshape(length, -1)
    return outputs * jax.nn.silu(gate_raw)


def bc_activate(bc_proj, kernel, offset_bias, segments):
    return jax.nn.silu(causal_conv(bc_proj, kernel, offset_bias, segments))


def keep_row(buffer, value, micro_index, in_range):
    updated = lax.dynamic_update_index_in_dim(buffer, value, micro_index, 0)
    return jnp.where(in_range, updated, buffer)


def pick_row(buffer, micro_index):
    return lax.dynamic_index_in_dim(buffer, micro_index, 0, keepdims=False)


def local(
    layer_input,
    segment_ids,
    out_cotangent,
    norm_gain,
    w_zx,
    w_bc,
    w_dt,
    conv_x,
    conv_x_bias,
    conv_bc,
    conv_bc_bias,
    dt_bias,
    a_log,
    d_skip,
    gate_gain,
    w_out,
):
    section_count = lax.axis_size("pipe")
    section_index = lax.axis_index("pipe")
    micro_count = layer_input.shape[0]
    row_count = layer_input.shape[2]
    model_width = layer_input.shape[3]
    length = segment_ids.shape[2]
    inner_local = w_zx.shape[3]
    bc_local = w_bc.shape[2]
    bc_width = bc_local * lax.axis_size("tensor")
    tick_count = micro_count + section_count - 1
    gain_in = norm_gain[0]
    w_cat = jnp.concatenate([w_zx[0, 0], w_zx[0, 1], w_bc[0], w_dt[0]], axis=1)
    column_count = w_cat.shape[1]
    kernel_x, offset_x = (conv_x[0], conv_x_bias[0])
    kernel_bc, offset_bc = (conv_bc[0], conv_bc_bias[0])
    step_bias, decay_log, skip_gain = (dt_bias[0], a_log[0], d_skip[0])
    input_rows = layer_input[:, 0]
    cotangent_rows = out_cotangent[:, 0]
    segment_rows = segment_ids[:, 0]
    mix_weight, mix_gain = (
        lax.all_gather(w_out[0], "tensor", axis=0, tiled=True),
        lax.all_gather(gate_gain[0], "tensor", axis=0, tiled=True),
    )
    gain_out = mix_gain.astype(jnp.float32)

    def split_columns(projected):
        return (
            projected[:, :inner_local],
            projected[:, inner_local : 2 * inner_local],
            projected[:, 2 * inner_local : 2 * inner_local + bc_local],
            projected[:, 2 * inner_local + bc_local :],
        )

    def forward(hidden_in, segments):
        hidden = hidden_in.astype(jnp.float32)
        row_scale = lax.rsqrt(jnp.mean(hidden * hidden, axis=-1, keepdims=True) + EPSILON)
        normed = (hidden * row_scale * gain_in).astype(jnp.bfloat16)
        gathered = lax.all_gather(normed, "tensor", axis=0, tiled=True)
        projected = jnp.dot(gathered, w_cat, preferred_element_type=jnp.float32)
        gate_raw, x_proj, bc_proj, step_raw = split_columns(projected)
        bc_part = bc_activate(bc_proj, kernel_bc, offset_bc, segments).astype(jnp.bfloat16)
        bc_values = lax.all_gather(bc_part, "tensor", axis=1, tiled=True)
        gated = mixer(
            x_proj,
            step_raw,
            bc_values.astype(jnp.float32),
            gate_raw,
            kernel_x,
            offset_x,
            step_bias,
            decay_log,
            skip_gain,
            segments,
            BLOCK,
        )
        gated_rows = lax.all_to_all(gated, "tensor", split_axis=0, concat_axis=1, tiled=True)
        gated_scale = lax.rsqrt(jnp.mean(gated_rows * gated_rows, axis=-1, keepdims=True) + EPSILON)
        normed_out = (gated_rows * gated_scale * gain_out).astype(jnp.bfloat16)
        mixer_out = jnp.dot(normed_out, mix_weight, preferred_element_type=jnp.float32)
        kept_values = (
            hidden_in,
            gathered,
            projected,
            bc_values,
            gated_rows,
            gated_scale,
            normed_out,
        )
        return ((hidden + mixer_out).astype(jnp.bfloat16), kept_values)

    def backward(grad_out, segments, kept_values):
        hidden_in, gathered, projected, bc_values = kept_values[:4]
        gate_raw, x_proj, bc_proj, step_raw = split_columns(projected)

        def local_mix(
            x_arg, step_arg, bc_arg, gate_arg, kernel_arg, offset_arg, bias_arg, decay_arg, skip_arg
        ):
            return mixer(
                x_arg,
                step_arg,
                bc_arg,
                gate_arg,
                kernel_arg,
                offset_arg,
                bias_arg,
                decay_arg,
                skip_arg,
                segments,
                BLOCK,
            )

        gated, mix_back = jax.vjp(
            local_mix,
            x_proj,
            step_raw,
            bc_values.astype(jnp.float32),
            gate_raw,
            kernel_x,
            offset_x,
            step_bias,
            decay_log,
            skip_gain,
        )
        gated_rows, gated_scale, normed_out = kept_values[4:]
        out_grad = jnp.dot(grad_out, mix_weight.T, preferred_element_type=jnp.float32)
        weight_grad = jnp.dot(normed_out.T, grad_out, preferred_element_type=jnp.float32)
        gain_grad = jnp.sum(out_grad * gated_rows * gated_scale, axis=0)
        scaled = out_grad * gain_out
        row_dots = jnp.mean(scaled * gated_rows, axis=-1, keepdims=True)
        row_grad = gated_scale * scaled - gated_rows * gated_scale**3 * row_dots
        gated_grad = lax.all_to_all(row_grad, "tensor", split_axis=1, concat_axis=0, tiled=True)
        (
            x_grad,
            step_grad,
            bc_grad,
            gate_grad,
            kernel_x_grad,
            offset_x_grad,
            bias_grad,
            decay_grad,
            skip_grad,
        ) = mix_back(gated_grad)
        bc_share = lax.psum_scatter(
            bc_grad.astype(jnp.bfloat16), "tensor", scatter_dimension=1, tiled=True
        ).astype(jnp.float32)
        _, bc_back = jax.vjp(
            lambda values, kernel, offset_bias: bc_activate(values, kernel, offset_bias, segments),
            bc_proj,
            kernel_bc,
            offset_bc,
        )
        bc_proj_grad, kernel_bc_grad, offset_bc_grad = bc_back(bc_share)
        proj_grad = jnp.concatenate([gate_grad, x_grad, bc_proj_grad, step_grad], axis=1).astype(
            jnp.bfloat16
        )
        cat_grad = jnp.dot(gathered.T, proj_grad, preferred_element_type=jnp.float32)
        normed_grad = lax.psum_scatter(
            jnp.dot(proj_grad, w_cat.T, preferred_element_type=jnp.float32).astype(jnp.bfloat16),
            "tensor",
            scatter_dimension=0,
            tiled=True,
        ).astype(jnp.float32)
        hidden = hidden_in.astype(jnp.float32)
        row_scale = lax.rsqrt(jnp.mean(hidden * hidden, axis=-1, keepdims=True) + EPSILON)
        in_gain_grad = jnp.sum(normed_grad * hidden * row_scale, axis=0)
        scaled_in = normed_grad * gain_in
        hidden_grad = row_scale * scaled_in - hidden * row_scale**3 * jnp.mean(
            scaled_in * hidden, axis=-1, keepdims=True
        )
        grad_in = (grad_out.astype(jnp.float32) + hidden_grad).astype(jnp.bfloat16)
        return (
            grad_in,
            (
                cat_grad,
                kernel_x_grad,
                offset_x_grad,
                kernel_bc_grad,
                offset_bc_grad,
                bias_grad,
                decay_grad,
                skip_grad,
                gain_grad,
                weight_grad,
                in_gain_grad,
            ),
        )

    kept_shapes = (
        ((row_count, model_width), jnp.bfloat16),
        ((length, model_width), jnp.bfloat16),
        ((length, column_count), jnp.float32),
        ((length, bc_width), jnp.bfloat16),
        ((row_count, INNER), jnp.float32),
        ((row_count, 1), jnp.float32),
        ((row_count, INNER), jnp.bfloat16),
    )
    kept_buffers = tuple(
        (jnp.zeros((micro_count,) + shape_pair[0], shape_pair[1]) for shape_pair in kept_shapes)
    )
    outputs_buffer = jnp.zeros((micro_count, row_count, model_width), jnp.bfloat16)

    def forward_tick(tick_number, carry):
        arrived, outputs_held, kept_held = carry
        micro_index = tick_number - section_index
        in_range = jnp.logical_and(micro_index >= 0, micro_index < micro_count)
        micro_index = jnp.clip(micro_index, 0, micro_count - 1)
        hidden_in = jnp.where(section_index == 0, pick_row(input_rows, micro_index), arrived)
        segments = pick_row(segment_rows, micro_index)
        result, kept_values = forward(hidden_in, segments)
        outputs_held = keep_row(outputs_held, result, micro_index, in_range)
        kept_held = jax.tree.map(
            lambda buffer, value: keep_row(buffer, value, micro_index, in_range),
            kept_held,
            kept_values,
        )
        arrived = shifted(result, "pipe", 1)
        return (arrived, outputs_held, kept_held)

    start_carry = (jnp.zeros((row_count, model_width), jnp.bfloat16), outputs_buffer, kept_buffers)
    _, outputs_buffer, kept_buffers = lax.fori_loop(0, tick_count, forward_tick, start_carry)
    grad_totals = tuple(
        (
            jnp.zeros(source.shape, jnp.float32)
            for source in (
                w_cat,
                kernel_x,
                offset_x,
                kernel_bc,
                offset_bc,
                step_bias,
                decay_log,
                skip_gain,
                mix_gain,
                mix_weight,
                gain_in,
            )
        )
    )
    grads_buffer = jnp.zeros((micro_count, row_count, model_width), jnp.bfloat16)

    def backward_tick(tick_number, carry):
        arrived, grads_held, totals_held = carry
        micro_index = tick_number - (section_count - 1 - section_index)
        in_range = jnp.logical_and(micro_index >= 0, micro_index < micro_count)
        micro_index = jnp.clip(micro_index, 0, micro_count - 1)
        grad_out = jnp.where(
            section_index == section_count - 1, pick_row(cotangent_rows, micro_index), arrived
        )
        segments = pick_row(segment_rows, micro_index)
        kept_values = jax.tree.map(lambda buffer: pick_row(buffer, micro_index), kept_buffers)
        grad_in, layer_grads = backward(grad_out, segments, kept_values)
        grads_held = keep_row(grads_held, grad_in, micro_index, in_range)
        totals_held = jax.tree.map(
            lambda summed, addend: summed + jnp.where(in_range, addend, 0.0),
            totals_held,
            layer_grads,
        )
        arrived = shifted(grad_in, "pipe", -1)
        return (arrived, grads_held, totals_held)

    start_back = (jnp.zeros((row_count, model_width), jnp.bfloat16), grads_buffer, grad_totals)
    _, grads_buffer, grad_totals = lax.fori_loop(0, tick_count, backward_tick, start_back)
    weight_total, gain_total = (
        lax.psum_scatter(
            grad_totals[9].astype(jnp.bfloat16), "tensor", scatter_dimension=0, tiled=True
        ).astype(jnp.float32),
        lax.psum_scatter(
            grad_totals[8].astype(jnp.bfloat16), "tensor", scatter_dimension=0, tiled=True
        ).astype(jnp.float32),
    )
    norm_total = lax.psum(grad_totals[10], "tensor")
    summed = (
        lax.psum(grad_totals[0].astype(jnp.bfloat16), "dp").astype(jnp.float32),
        lax.psum(grad_totals[1].astype(jnp.bfloat16), "dp").astype(jnp.float32),
        lax.psum(grad_totals[2].astype(jnp.bfloat16), "dp").astype(jnp.float32),
        lax.psum(grad_totals[3].astype(jnp.bfloat16), "dp").astype(jnp.float32),
        lax.psum(grad_totals[4].astype(jnp.bfloat16), "dp").astype(jnp.float32),
        lax.psum(grad_totals[5].astype(jnp.bfloat16), "dp").astype(jnp.float32),
        lax.psum(grad_totals[6].astype(jnp.bfloat16), "dp").astype(jnp.float32),
        lax.psum(grad_totals[7].astype(jnp.bfloat16), "dp").astype(jnp.float32),
        lax.psum(gain_total.astype(jnp.bfloat16), "dp").astype(jnp.float32),
        lax.psum(weight_total.astype(jnp.bfloat16), "dp").astype(jnp.float32),
        lax.psum(norm_total.astype(jnp.bfloat16), "dp").astype(jnp.float32),
    )
    cat_total = summed[0]
    grad_zx = jnp.stack([cat_total[:, :inner_local], cat_total[:, inner_local : 2 * inner_local]])[
        None
    ]
    grad_bc = cat_total[:, 2 * inner_local : 2 * inner_local + bc_local][None]
    grad_dt = cat_total[:, 2 * inner_local + bc_local :][None]
    return (
        outputs_buffer[None, :, None],
        grads_buffer[None, :, None],
        summed[10][None],
        grad_zx,
        grad_bc,
        grad_dt,
        summed[1][None],
        summed[2][None],
        summed[3][None],
        summed[4][None],
        summed[5][None],
        summed[6][None],
        summed[7][None],
        summed[8][None],
        summed[9][None],
    )


def solution(mesh):
    return jax.shard_map(
        local,
        mesh=mesh,
        in_specs=(
            P(None, "dp", "tensor", None),
            P(None, "dp", None),
            P(None, "dp", "tensor", None),
            P("pipe", None),
            P("pipe", None, None, "tensor"),
            P("pipe", None, "tensor"),
            P("pipe", None, "tensor"),
            P("pipe", None, "tensor"),
            P("pipe", "tensor"),
            P("pipe", None, "tensor"),
            P("pipe", "tensor"),
            P("pipe", "tensor"),
            P("pipe", "tensor"),
            P("pipe", "tensor"),
            P("pipe", "tensor"),
            P("pipe", "tensor", None),
        ),
        out_specs=(
            P("pipe", None, "dp", "tensor", None),
            P("pipe", None, "dp", "tensor", None),
            P("pipe", None),
            P("pipe", None, None, "tensor"),
            P("pipe", None, "tensor"),
            P("pipe", None, "tensor"),
            P("pipe", None, "tensor"),
            P("pipe", "tensor"),
            P("pipe", None, "tensor"),
            P("pipe", "tensor"),
            P("pipe", "tensor"),
            P("pipe", "tensor"),
            P("pipe", "tensor"),
            P("pipe", "tensor"),
            P("pipe", "tensor", None),
        ),
        check_vma=False,
    )
```

profile of v0, /device:TPU:0, one launch (start us, length us, event | category | flops | bytes accessed | tf_op | source)
XLA Modules:
  0.0 1843.4 jit_solution(14548824456078127101)
XLA Ops:
  11.3 13.8 all-gather
  28.2 31.3 %all-gather.5.cloned.1.call-done = bf16[1,2048,1024]{2,1,0:T(8,128)(2,1)} async-done(((bf16[1,256,1024]{2,1,0:T(8,128)(2,1)}), bf16[1,2048,1024]{2,1,0:T(8,128)(2,1)}) %all-gather.5.cloned.1.call-update) | async-done | bytes 4194320 | tf_op jit(solution)/shard_map/all_gather | solution.py:160
  77.4 635.6 %while.71 = (s32[]{:T(128)}, bf16[128,1024]{1,0:T(8,128)(2,1)}, bf16[4,128,1024]{2,1,0:T(8,128)(2,1)}, bf16[4,128,1024]{2,1,0:T(8,128)(2,1)}, bf16[4,1024,1024]{...) while((s32[]{:T(128)}, bf16[128,1024]{1,0:T(8,128)(2,1)}, ...), condition=%wide.region_5.6_spmd, body=%wide.region_0.5_spmd.sunk | while | flops 3388336640 | bytes 101023200 | solution.py:339
  89.2 20.2 %all-gather.7.cloned.1.call-done = bf16[1024,1024]{1,0:T(8,128)(2,1)} async-done(((bf16[128,1024]{1,0:T(8,128)(2,1)}), bf16[1024,1024]{1,0:T(8,128)(2,1)}) %all-gather.7.cloned.1.call-update) | async-done | bytes 2097168 | tf_op jit(solution)/shard_map/while/body/eval_jaxpr/all_gather | solution.py:177
  122.0 14.8 all_gather.31
  170.0 20.4 %all-to-all-done = f32[8,128,256]{1,2,0:T(8,128)S(1)} async-done(((f32[8,128,256]{1,2,0:T(8,128)}), f32[8,128,256]{1,2,0:T(8,128)S(1)}, u32[]{:S(2)}, u32[]{:S(2)}) %all-to-all-start) | async-done | bytes 1048608 | tf_op jit(solution)/shard_map/while/body/eval_jaxpr/all_to_all | solution.py:195
  215.8 20.8 %all-gather.7.cloned.1.call-done = bf16[1024,1024]{1,0:T(8,128)(2,1)} async-done(((bf16[128,1024]{1,0:T(8,128)(2,1)}), bf16[1024,1024]{1,0:T(8,128)(2,1)}) %all-gather.7.cloned.1.call-update) | async-done | bytes 2097168 | tf_op jit(solution)/shard_map/while/body/eval_jaxpr/all_gather | solution.py:177
  249.2 14.6 all_gather.31
  297.0 20.4 %all-to-all-done = f32[8,128,256]{1,2,0:T(8,128)S(1)} async-done(((f32[8,128,256]{1,2,0:T(8,128)}), f32[8,128,256]{1,2,0:T(8,128)S(1)}, u32[]{:S(2)}, u32[]{:S(2)}) %all-to-all-start) | async-done | bytes 1048608 | tf_op jit(solution)/shard_map/while/body/eval_jaxpr/all_to_all | solution.py:195
  342.9 20.8 %all-gather.7.cloned.1.call-done = bf16[1024,1024]{1,0:T(8,128)(2,1)} async-done(((bf16[128,1024]{1,0:T(8,128)(2,1)}), bf16[1024,1024]{1,0:T(8,128)(2,1)}) %all-gather.7.cloned.1.call-update) | async-done | bytes 2097168 | tf_op jit(solution)/shard_map/while/body/eval_jaxpr/all_gather | solution.py:177
  376.4 14.6 all_gather.31
  424.2 20.4 %all-to-all-done = f32[8,128,256]{1,2,0:T(8,128)S(1)} async-done(((f32[8,128,256]{1,2,0:T(8,128)}), f32[8,128,256]{1,2,0:T(8,128)S(1)}, u32[]{:S(2)}, u32[]{:S(2)}) %all-to-all-start) | async-done | bytes 1048608 | tf_op jit(solution)/shard_map/while/body/eval_jaxpr/all_to_all | solution.py:195
  470.2 20.7 %all-gather.7.cloned.1.call-done = bf16[1024,1024]{1,0:T(8,128)(2,1)} async-done(((bf16[128,1024]{1,0:T(8,128)(2,1)}), bf16[1024,1024]{1,0:T(8,128)(2,1)}) %all-gather.7.cloned.1.call-update) | async-done | bytes 2097168 | tf_op jit(solution)/shard_map/while/body/eval_jaxpr/all_gather | solution.py:177
  503.5 14.6 all_gather.31
  551.3 20.4 %all-to-all-done = f32[8,128,256]{1,2,0:T(8,128)S(1)} async-done(((f32[8,128,256]{1,2,0:T(8,128)}), f32[8,128,256]{1,2,0:T(8,128)S(1)}, u32[]{:S(2)}, u32[]{:S(2)}) %all-to-all-start) | async-done | bytes 1048608 | tf_op jit(solution)/shard_map/while/body/eval_jaxpr/all_to_all | solution.py:195
  597.3 20.8 %all-gather.7.cloned.1.call-done = bf16[1024,1024]{1,0:T(8,128)(2,1)} async-done(((bf16[128,1024]{1,0:T(8,128)(2,1)}), bf16[1024,1024]{1,0:T(8,128)(2,1)}) %all-gather.7.cloned.1.call-update) | async-done | bytes 2097168 | tf_op jit(solution)/shard_map/while/body/eval_jaxpr/all_gather | solution.py:177
  630.7 14.8 all_gather.31
  678.6 20.4 %all-to-all-done = f32[8,128,256]{1,2,0:T(8,128)S(1)} async-done(((f32[8,128,256]{1,2,0:T(8,128)}), f32[8,128,256]{1,2,0:T(8,128)S(1)}, u32[]{:S(2)}, u32[]{:S(2)}) %all-to-all-start) | async-done | bytes 1048608 | tf_op jit(solution)/shard_map/while/body/eval_jaxpr/all_to_all | solution.py:195
  714.2 1006.9 %while.72 = (s32[]{:T(128)}, bf16[128,1024]{1,0:T(8,128)(2,1)S(1)}, bf16[4,128,1024]{2,1,0:T(8,128)(2,1)}, f32[1024,548]{0,1:T(8,128)}, f32[4,256]{1,0:T(4,128)}...) while((s32[]{:T(128)}, bf16[128,1024]{1,0:T(8,128)(2,1)S(1)}, ...), condition=%wide.region_42.43_spmd.clone, body=%wide.region_6.42_spmd.clone.sunk | while | flops 9152633856 | bytes 222797360 | solution.py:381
  818.6 20.8 %reduce-window.78 = f32[4,4,2,128]{3,2,1,0:T(2,128)S(1)} reduce-window(f32[4,4,2,128]{3,2,1,0:T(2,128)} %reshape.1049, f32[]{:T(128)} %constant.394.clone.1..sunk.1), window={size=1x1x1x128 pad=0_0x0_0x0_0x0_127}, to_apply=%region_22.22 | reduce-window | flops 520192 | bytes 32772 | tf_op jit(solution)/shard_map/reduce-window.34
  852.1 7.4 fusion.383
  871.8 10.1 reduce-scatter.6.cloned.1.call-done
  900.4 22.2 %reduce-scatter.8.cloned.1.call-done = bf16[128,1024]{1,0:T(8,128)(2,1)} async-done(((bf16[1024,1024]{1,0:T(8,128)(2,1)}), bf16[128,1024]{1,0:T(8,128)(2,1)}) %reduce-scatter.8.cloned.1.call-update) | async-done | bytes 262160 | tf_op jit(solution)/shard_map/while/body/eval_jaxpr/reduce_scatter | solution.py:276
  1015.6 20.8 %reduce-window.78 = f32[4,4,2,128]{3,2,1,0:T(2,128)S(1)} reduce-window(f32[4,4,2,128]{3,2,1,0:T(2,128)} %reshape.1049, f32[]{:T(128)} %constant.394.clone.1..sunk.1), window={size=1x1x1x128 pad=0_0x0_0x0_0x0_127}, to_apply=%region_22.22 | reduce-window | flops 520192 | bytes 32772 | tf_op jit(solution)/shard_map/reduce-window.34
  1049.0 7.4 fusion.383
  1068.8 9.2 reduce-scatter.6.cloned.1.call-done
  1085.9 8.4 select_add_fusion.19
  1099.8 18.7 %reduce-scatter.8.cloned.1.call-done = bf16[128,1024]{1,0:T(8,128)(2,1)} async-done(((bf16[1024,1024]{1,0:T(8,128)(2,1)}), bf16[128,1024]{1,0:T(8,128)(2,1)}) %reduce-scatter.8.cloned.1.call-update) | async-done | bytes 262160 | tf_op jit(solution)/shard_map/while/body/eval_jaxpr/reduce_scatter | solution.py:276
  1211.5 20.8 %reduce-window.78 = f32[4,4,2,128]{3,2,1,0:T(2,128)S(1)} reduce-window(f32[4,4,2,128]{3,2,1,0:T(2,128)} %reshape.1049, f32[]{:T(128)} %constant.394.clone.1..sunk.1), window={size=1x1x1x128 pad=0_0x0_0x0_0x0_127}, to_apply=%region_22.22 | reduce-window | flops 520192 | bytes 32772 | tf_op jit(solution)/shard_map/reduce-window.34
  1245.0 7.4 fusion.383
  1264.7 9.3 reduce-scatter.6.cloned.1.call-done
  1281.9 8.4 select_add_fusion.19
  1295.9 18.8 %reduce-scatter.8.cloned.1.call-done = bf16[128,1024]{1,0:T(8,128)(2,1)} async-done(((bf16[1024,1024]{1,0:T(8,128)(2,1)}), bf16[128,1024]{1,0:T(8,128)(2,1)}) %reduce-scatter.8.cloned.1.call-update) | async-done | bytes 262160 | tf_op jit(solution)/shard_map/while/body/eval_jaxpr/reduce_scatter | solution.py:276
  1407.5 20.8 %reduce-window.78 = f32[4,4,2,128]{3,2,1,0:T(2,128)S(1)} reduce-window(f32[4,4,2,128]{3,2,1,0:T(2,128)} %reshape.1049, f32[]{:T(128)} %constant.394.clone.1..sunk.1), window={size=1x1x1x128 pad=0_0x0_0x0_0x0_127}, to_apply=%region_22.22 | reduce-window | flops 520192 | bytes 32772 | tf_op jit(solution)/shard_map/reduce-window.34
  1441.0 7.4 fusion.383
  1460.8 9.5 reduce-scatter.6.cloned.1.call-done
  1478.1 8.4 select_add_fusion.19
  1492.1 18.5 %reduce-scatter.8.cloned.1.call-done = bf16[128,1024]{1,0:T(8,128)(2,1)} async-done(((bf16[1024,1024]{1,0:T(8,128)(2,1)}), bf16[128,1024]{1,0:T(8,128)(2,1)}) %reduce-scatter.8.cloned.1.call-update) | async-done | bytes 262160 | tf_op jit(solution)/shard_map/while/body/eval_jaxpr/reduce_scatter | solution.py:276
  1603.5 20.8 %reduce-window.78 = f32[4,4,2,128]{3,2,1,0:T(2,128)S(1)} reduce-window(f32[4,4,2,128]{3,2,1,0:T(2,128)} %reshape.1049, f32[]{:T(128)} %constant.394.clone.1..sunk.1), window={size=1x1x1x128 pad=0_0x0_0x0_0x0_127}, to_apply=%region_22.22 | reduce-window | flops 520192 | bytes 32772 | tf_op jit(solution)/shard_map/reduce-window.34
  1637.0 7.4 fusion.383
  1656.7 9.5 reduce-scatter.6.cloned.1.call-done
  1674.1 8.4 select_add_fusion.19
  1688.0 18.7 %reduce-scatter.8.cloned.1.call-done = bf16[128,1024]{1,0:T(8,128)(2,1)} async-done(((bf16[1024,1024]{1,0:T(8,128)(2,1)}), bf16[128,1024]{1,0:T(8,128)(2,1)}) %reduce-scatter.8.cloned.1.call-update) | async-done | bytes 262160 | tf_op jit(solution)/shard_map/while/body/eval_jaxpr/reduce_scatter | solution.py:276
  1730.0 45.7 %reduce-scatter.4.cloned.1.call-done = bf16[256,1024]{1,0:T(8,128)(2,1)} async-done(((bf16[2048,1024]{1,0:T(8,128)(2,1)}), bf16[256,1024]{1,0:T(8,128)(2,1)}) %reduce-scatter.4.cloned.1.call-update) | async-done | bytes 524304 | tf_op jit(solution)/shard_map/reduce_scatter | solution.py:383
  1777.0 13.8 psum.84
  1790.8 13.6 all-reduce.31
  1804.6 8.2 all-reduce.32
  1817.7 12.5 all-reduce.36.cloned.1.call-done
  (1930 shorter events, 1058.4 us)
Async XLA Ops:
  7.2 52.3 %all-gather.5.cloned.1.call-start = ((), (), s32[]{:S(2)}) async-start(), calls=%async_computation.6 | async-start | bytes 4718592 | tf_op jit(solution)/shard_map/all_gather | solution.py:160
  77.8 31.6 %all-gather.7.cloned.1.call-start = ((), (), s32[]{:S(2)}) async-start(), calls=%async_computation.8 | async-start | bytes 2359296 | tf_op jit(solution)/shard_map/while/body/eval_jaxpr/all_gather | solution.py:177
  160.2 30.2 %all-to-all-start = ((f32[8,128,256]{1,2,0:T(8,128)}), f32[8,128,256]{1,2,0:T(8,128)S(1)}, u32[]{:S(2)}, u32[]{:S(2)}) async-start(f32[8,128,256]{1,2,0:T(8,128)} %copy_bitcast_fusion.4), calls=%async_computation | async-start | bytes 2097152 | tf_op jit(solution)/shard_map/while/body/eval_jaxpr/all_to_all | solution.py:195
  194.7 9.7 collective-permute-start
  204.4 32.1 %all-gather.7.cloned.1.call-start = ((), (), s32[]{:S(2)}) async-start(), calls=%async_computation.8 | async-start | bytes 2359296 | tf_op jit(solution)/shard_map/while/body/eval_jaxpr/all_gather | solution.py:177
  287.2 30.2 %all-to-all-start = ((f32[8,128,256]{1,2,0:T(8,128)}), f32[8,128,256]{1,2,0:T(8,128)S(1)}, u32[]{:S(2)}, u32[]{:S(2)}) async-start(f32[8,128,256]{1,2,0:T(8,128)} %copy_bitcast_fusion.4), calls=%async_computation | async-start | bytes 2097152 | tf_op jit(solution)/shard_map/while/body/eval_jaxpr/all_to_all | solution.py:195
  321.8 9.8 collective-permute-start
  331.6 32.2 %all-gather.7.cloned.1.call-start = ((), (), s32[]{:S(2)}) async-start(), calls=%async_computation.8 | async-start | bytes 2359296 | tf_op jit(solution)/shard_map/while/body/eval_jaxpr/all_gather | solution.py:177
  414.4 30.2 %all-to-all-start = ((f32[8,128,256]{1,2,0:T(8,128)}), f32[8,128,256]{1,2,0:T(8,128)S(1)}, u32[]{:S(2)}, u32[]{:S(2)}) async-start(f32[8,128,256]{1,2,0:T(8,128)} %copy_bitcast_fusion.4), calls=%async_computation | async-start | bytes 2097152 | tf_op jit(solution)/shard_map/while/body/eval_jaxpr/all_to_all | solution.py:195
  448.9 9.8 collective-permute-start
  458.8 32.1 %all-gather.7.cloned.1.call-start = ((), (), s32[]{:S(2)}) async-start(), calls=%async_computation.8 | async-start | bytes 2359296 | tf_op jit(solution)/shard_map/while/body/eval_jaxpr/all_gather | solution.py:177
  541.5 30.2 %all-to-all-start = ((f32[8,128,256]{1,2,0:T(8,128)}), f32[8,128,256]{1,2,0:T(8,128)S(1)}, u32[]{:S(2)}, u32[]{:S(2)}) async-start(f32[8,128,256]{1,2,0:T(8,128)} %copy_bitcast_fusion.4), calls=%async_computation | async-start | bytes 2097152 | tf_op jit(solution)/shard_map/while/body/eval_jaxpr/all_to_all | solution.py:195
  576.1 9.8 collective-permute-start
  585.9 32.1 %all-gather.7.cloned.1.call-start = ((), (), s32[]{:S(2)}) async-start(), calls=%async_computation.8 | async-start | bytes 2359296 | tf_op jit(solution)/shard_map/while/body/eval_jaxpr/all_gather | solution.py:177
  668.8 30.2 %all-to-all-start = ((f32[8,128,256]{1,2,0:T(8,128)}), f32[8,128,256]{1,2,0:T(8,128)S(1)}, u32[]{:S(2)}, u32[]{:S(2)}) async-start(f32[8,128,256]{1,2,0:T(8,128)} %copy_bitcast_fusion.4), calls=%async_computation | async-start | bytes 2097152 | tf_op jit(solution)/shard_map/while/body/eval_jaxpr/all_to_all | solution.py:195
  703.4 9.7 collective-permute-start
  746.6 30.8 %all-to-all-start.1 = ((f32[128,8,256]{2,0,1:T(8,128)}), f32[128,8,256]{2,0,1:T(8,128)}, u32[]{:S(2)}, u32[]{:S(2)}) async-start(f32[128,8,256]{2,0,1:T(8,128)} %bitcast.650), calls=%async_computation.1 | async-start | bytes 2097152 | tf_op jit(solution)/shard_map/while/body/eval_jaxpr/all_to_all | solution.py:250
  750.8 131.2 %reduce-scatter.6.cloned.1.call-start = ((), (), s32[]{:S(2)}) async-start(), calls=%async_computation.9 | async-start | bytes 589824 | tf_op jit(solution)/shard_map/while/body/eval_jaxpr/reduce_scatter | solution.py:262
  852.0 70.6 %reduce-scatter.8.cloned.1.call-start = ((), (), s32[]{:S(2)}) async-start(), calls=%async_computation.10 | async-start | bytes 2359296 | tf_op jit(solution)/shard_map/while/body/eval_jaxpr/reduce_scatter | solution.py:276
  926.0 8.3 collective-permute-start.1
  943.5 30.8 %all-to-all-start.1 = ((f32[128,8,256]{2,0,1:T(8,128)}), f32[128,8,256]{2,0,1:T(8,128)}, u32[]{:S(2)}, u32[]{:S(2)}) async-start(f32[128,8,256]{2,0,1:T(8,128)} %bitcast.650), calls=%async_computation.1 | async-start | bytes 2097152 | tf_op jit(solution)/shard_map/while/body/eval_jaxpr/all_to_all | solution.py:250
  947.8 130.2 %reduce-scatter.6.cloned.1.call-start = ((), (), s32[]{:S(2)}) async-start(), calls=%async_computation.9 | async-start | bytes 589824 | tf_op jit(solution)/shard_map/while/body/eval_jaxpr/reduce_scatter | solution.py:262
  1049.0 69.6 %reduce-scatter.8.cloned.1.call-start = ((), (), s32[]{:S(2)}) async-start(), calls=%async_computation.10 | async-start | bytes 2359296 | tf_op jit(solution)/shard_map/while/body/eval_jaxpr/reduce_scatter | solution.py:276
  1121.9 8.3 collective-permute-start.1
  1139.4 30.8 %all-to-all-start.1 = ((f32[128,8,256]{2,0,1:T(8,128)}), f32[128,8,256]{2,0,1:T(8,128)}, u32[]{:S(2)}, u32[]{:S(2)}) async-start(f32[128,8,256]{2,0,1:T(8,128)} %bitcast.650), calls=%async_computation.1 | async-start | bytes 2097152 | tf_op jit(solution)/shard_map/while/body/eval_jaxpr/all_to_all | solution.py:250
  1143.7 130.3 %reduce-scatter.6.cloned.1.call-start = ((), (), s32[]{:S(2)}) async-start(), calls=%async_computation.9 | async-start | bytes 589824 | tf_op jit(solution)/shard_map/while/body/eval_jaxpr/reduce_scatter | solution.py:262
  1244.9 69.7 %reduce-scatter.8.cloned.1.call-start = ((), (), s32[]{:S(2)}) async-start(), calls=%async_computation.10 | async-start | bytes 2359296 | tf_op jit(solution)/shard_map/while/body/eval_jaxpr/reduce_scatter | solution.py:276
  1318.0 8.3 collective-permute-start.1
  1335.5 30.8 %all-to-all-start.1 = ((f32[128,8,256]{2,0,1:T(8,128)}), f32[128,8,256]{2,0,1:T(8,128)}, u32[]{:S(2)}, u32[]{:S(2)}) async-start(f32[128,8,256]{2,0,1:T(8,128)} %bitcast.650), calls=%async_computation.1 | async-start | bytes 2097152 | tf_op jit(solution)/shard_map/while/body/eval_jaxpr/all_to_all | solution.py:250
  1339.8 130.5 %reduce-scatter.6.cloned.1.call-start = ((), (), s32[]{:S(2)}) async-start(), calls=%async_computation.9 | async-start | bytes 589824 | tf_op jit(solution)/shard_map/while/body/eval_jaxpr/reduce_scatter | solution.py:262
  1441.0 69.6 %reduce-scatter.8.cloned.1.call-start = ((), (), s32[]{:S(2)}) async-start(), calls=%async_computation.10 | async-start | bytes 2359296 | tf_op jit(solution)/shard_map/while/body/eval_jaxpr/reduce_scatter | solution.py:276
  1513.9 8.3 collective-permute-start.1
  1531.5 30.8 %all-to-all-start.1 = ((f32[128,8,256]{2,0,1:T(8,128)}), f32[128,8,256]{2,0,1:T(8,128)}, u32[]{:S(2)}, u32[]{:S(2)}) async-start(f32[128,8,256]{2,0,1:T(8,128)} %bitcast.650), calls=%async_computation.1 | async-start | bytes 2097152 | tf_op jit(solution)/shard_map/while/body/eval_jaxpr/all_to_all | solution.py:250
  1535.7 130.5 %reduce-scatter.6.cloned.1.call-start = ((), (), s32[]{:S(2)}) async-start(), calls=%async_computation.9 | async-start | bytes 589824 | tf_op jit(solution)/shard_map/while/body/eval_jaxpr/reduce_scatter | solution.py:262
  1636.9 69.8 %reduce-scatter.8.cloned.1.call-start = ((), (), s32[]{:S(2)}) async-start(), calls=%async_computation.10 | async-start | bytes 2359296 | tf_op jit(solution)/shard_map/while/body/eval_jaxpr/reduce_scatter | solution.py:276
  1710.1 8.3 collective-permute-start.1
  1721.1 54.6 %reduce-scatter.4.cloned.1.call-start = ((), (), s32[]{:S(2)}) async-start(), calls=%async_computation.5 | async-start | bytes 4718592 | tf_op jit(solution)/shard_map/reduce_scatter | solution.py:383
  1727.2 103.0 %all-reduce.36.cloned.1.call-start = ((), (), s32[]{:S(2)}) async-start(), calls=%async_computation.7 | async-start | bytes 3309568 | tf_op jit(solution)/shard_map/psum | solution.py:392
  1728.8 47.0 %copy-start.105 = (u32[32]{0:T(128)S(1)}, u32[32]{0:T(128)}, u32[]{:S(2)}) copy-start(u32[32]{0:T(128)} %constant.478) | copy-start | bytes 388
  1728.8 48.2 %copy-start.64 = (f32[1024]{0:T(1024)S(1)}, f32[1024]{0:T(1024)}, u32[]{:S(2)}) copy-start(f32[1024]{0:T(1024)} %get-tuple-element.1408) | copy-start | bytes 12292
  1728.8 62.0 %copy-start.89 = (f32[256]{0:T(256)S(1)}, f32[256]{0:T(256)}, u32[]{:S(2)}) copy-start(f32[256]{0:T(256)} %get-tuple-element.1411) | copy-start | bytes 3076
  1728.8 62.0 %copy-start.41 = (f32[2048]{0:T(1024)S(1)}, f32[2048]{0:T(1024)}, u32[]{:S(2)}) copy-start(f32[2048]{0:T(1024)} %get-tuple-element.1417) | copy-start | bytes 24580
  1728.8 75.7 %copy-start.100 = (f32[32]{0:T(128)S(1)}, f32[32]{0:T(128)}, u32[]{:S(2)}) copy-start(f32[32]{0:T(128)} %get-tuple-element.1413) | copy-start | bytes 388
  1728.8 75.7 %copy-start.103 = (f32[4]{0:T(128)S(1)}, f32[4]{0:T(128)}, u32[]{:S(2)}) copy-start(f32[4]{0:T(128)} %get-tuple-element.1414) | copy-start | bytes 52
  1728.8 75.7 %copy-start.92 = (f32[4]{0:T(128)S(1)}, f32[4]{0:T(128)}, u32[]{:S(2)}) copy-start(f32[4]{0:T(128)} %get-tuple-element.1415) | copy-start | bytes 52
  1728.8 75.7 %copy-start.95 = (f32[4]{0:T(128)S(1)}, f32[4]{0:T(128)}, u32[]{:S(2)}) copy-start(f32[4]{0:T(128)} %get-tuple-element.1416) | copy-start | bytes 52
  1728.8 75.8 %copy-start.84 = (f32[4,32]{1,0:T(4,128)S(1)}, f32[4,32]{1,0:T(4,128)}, u32[]{:S(2)}) copy-start(f32[4,32]{1,0:T(4,128)} %get-tuple-element.1412) | copy-start | bytes 1540
  1728.8 75.8 %copy-start.61 = (f32[4,256]{1,0:T(4,128)S(1)}, f32[4,256]{1,0:T(4,128)}, u32[]{:S(2)}) copy-start(f32[4,256]{1,0:T(4,128)} %get-tuple-element.1410) | copy-start | bytes 12292
  (452 other events, 4101.2 us)
Sparse Core Ops, SparseCore 0:
  9.6 49.8 all-gather.4
  81.5 27.9 all-gather.6
  208.1 28.4 all-gather.6
  335.2 28.4 all-gather.6
  462.4 28.4 all-gather.6
  589.5 28.4 all-gather.6
  852.1 29.8 reduce-scatter.5
  888.6 33.9 reduce-scatter.7
  1049.1 28.8 reduce-scatter.5
  1084.7 33.8 reduce-scatter.7
  1245.0 28.9 reduce-scatter.5
  1280.7 33.9 reduce-scatter.7
  1441.1 29.1 reduce-scatter.5
  1476.9 33.6 reduce-scatter.7
  1637.0 29.1 reduce-scatter.5
  1672.8 33.8 reduce-scatter.7
  1727.3 48.3 reduce-scatter.3
  1778.5 51.6 all-reduce.35
where the time goes:
time: 1850 us; the launch traced here: 1840 us
  waiting for transfers between devices  493 us (27%)
  other arithmetic  436 us (24%)
  matrix products  399 us (22%)
  local copies, waits for them, and re-layouts  277 us (15%)
  blocking collectives  123 us (7%)
  starting transfers between devices  67.1 us (4%)
  loops' own time  33.3 us (2%)
    another operation x60, other arithmetic  167 us
    dot_general x20, matrix products, state_scan(): jnp.einsum('chts,cshp->cthp', affinity[:, None] * decays, weighted, preci...  125 us
    all_gather x5, waiting for transfers between devices, forward(): gathered = lax.all_gather(normed, 'tensor', axis=0, tiled=True)  103 us
    all_to_all x5, waiting for transfers between devices, forward(): lax.all_to_all(gated, 'tensor', split_axis=0, concat_axis=1, tiled=True)  102 us
    reduce_scatter x5, waiting for transfers between devices, backward(): lax.psum_scatter(jnp.dot(proj_grad, w_cat.T, preferred_element_type=jnp.f...  96.9 us
    select_n x35, other arithmetic, keep_row(): return jnp.where(in_range, updated, buffer)  78.7 us
    all_gather x5, blocking collectives, forward(): bc_values = lax.all_gather(bc_part, 'tensor', axis=1, tiled=True)  73.4 us
    dynamic_slice x40, local copies, waits for them, and re-layouts, pick_row(): return lax.dynamic_index_in_dim(buffer, micro_index, 0, keepdims=False)  48.6 us
  transfers between devices with their start and end apart: 38, of which 33 were waited for; matrix products, arithmetic and copies ran while one was open for 21% of the time, Pallas kernels for 0%

commit v1 on v0

v1 whole, which is shorter than its diff:
```python
import jax
import jax.numpy as jnp
from jax import lax
from jax.sharding import PartitionSpec as P

BLOCK = 256


EPSILON = 1e-05
PRECISE = lax.Precision.HIGH


def causal_conv(values, kernel, offset_bias, segments):
    taps_count = kernel.shape[0]
    length = values.shape[0]
    padded = jnp.pad(values, ((taps_count - 1, 0), (0, 0)))
    padded_ids = jnp.pad(segments, (taps_count - 1, 0), constant_values=-1)
    result = jnp.zeros_like(values) + offset_bias
    for offset in range(taps_count):
        first_row = taps_count - 1 - offset
        earlier = padded[first_row : first_row + length]
        same_doc = (padded_ids[first_row : first_row + length] == segments).astype(values.dtype)
        result = result + kernel[offset] * earlier * same_doc[:, None]
    return result


def state_scan(inputs, step_sizes, decay_rates, b_values, c_values, segments, block_size):
    length, head_count, head_width = inputs.shape
    blocks = length // block_size
    state_count = b_values.shape[1]
    log_decay = (step_sizes * decay_rates).reshape(blocks, block_size, head_count)
    lower_mask = jnp.tril(jnp.ones((block_size, block_size), inputs.dtype))
    cumul = jnp.einsum(
        "ts,csh->cth", lower_mask, log_decay, precision=lax.Precision.HIGHEST
    )
    weighted = (inputs * step_sizes[:, :, None]).reshape(blocks, block_size, head_count, head_width)
    b_blocks = b_values.reshape(blocks, block_size, state_count)
    c_blocks = c_values.reshape(blocks, block_size, state_count)
    block_ids = segments.reshape(blocks, block_size)
    same_doc = (block_ids[:, :, None] == block_ids[:, None, :]).astype(inputs.dtype) * lower_mask
    cumul_heads = jnp.transpose(cumul, (0, 2, 1))
    log_gaps = cumul_heads[:, :, :, None] - cumul_heads[:, :, None, :]
    mask_heads = same_doc[:, None]
    decays = jnp.exp(jnp.where(mask_heads > 0, log_gaps, 0.0)) * mask_heads
    affinity = jnp.einsum("ctn,csn->cts", c_blocks, b_blocks)
    inside = jnp.einsum("chts,cshp->cthp", affinity[:, None] * decays, weighted, precision=PRECISE)
    ending = cumul[:, -1, :]
    to_end = (
        jnp.exp(ending[:, None, :] - cumul)
        * (block_ids == block_ids[:, -1:]).astype(inputs.dtype)[:, :, None]
    )
    block_states = jnp.einsum(
        "csn,cshp->chnp", b_blocks, weighted * to_end[:, :, :, None], precision=PRECISE
    )
    before = jnp.concatenate([jnp.full((1,), -1, jnp.int32), block_ids[:-1, -1]])
    carry_keep = jnp.exp(ending) * (block_ids[:, -1] == before).astype(inputs.dtype)[:, None]
    running = jnp.zeros_like(block_states[0])
    entering = []
    for block_index in range(blocks):
        entering.append(running)
        running = carry_keep[block_index][:, None, None] * running + block_states[block_index]
    entering = jnp.stack(entering)
    from_start = jnp.exp(cumul) * (block_ids == before[:, None]).astype(inputs.dtype)[:, :, None]
    across = (
        jnp.einsum("ctn,chnp->cthp", c_blocks, entering, precision=PRECISE)
        * from_start[:, :, :, None]
    )
    return (inside + across).reshape(length, head_count, head_width)


def mixer(
    x_proj,
    step_raw,
    bc_values,
    gate_raw,
    kernel_x,
    offset_x,
    step_bias,
    decay_log,
    skip_gain,
    segments,
    block_size,
):
    mixed_in = jax.nn.silu(causal_conv(x_proj, kernel_x, offset_x, segments))
    length = x_proj.shape[0]
    head_count = step_raw.shape[1]
    step_sizes = jax.nn.softplus(step_raw + step_bias)
    decay_rates = -jnp.exp(decay_log)
    state_count = bc_values.shape[1] // 2
    per_head = mixed_in.reshape(length, head_count, -1)
    scanned = state_scan(
        per_head,
        step_sizes,
        decay_rates,
        bc_values[:, :state_count],
        bc_values[:, state_count:],
        segments,
        block_size,
    )
    outputs = (scanned + skip_gain[None, :, None] * per_head).reshape(length, -1)
    return outputs * jax.nn.silu(gate_raw)


def bc_activate(bc_proj, kernel, offset_bias, segments):
    return jax.nn.silu(causal_conv(bc_proj, kernel, offset_bias, segments))


def local(
    layer_input,
    segment_ids,
    out_cotangent,
    norm_gain,
    w_zx,
    w_bc,
    w_dt,
    conv_x,
    conv_x_bias,
    conv_bc,
    conv_bc_bias,
    dt_bias,
    a_log,
    d_skip,
    gate_gain,
    w_out,
):
    section_count = lax.axis_size("pipe")
    section_index = lax.axis_index("pipe")
    shard_count = lax.axis_size("tensor")
    shard_index = lax.axis_index("tensor")
    micro_count = layer_input.shape[0]
    micro_local = micro_count // section_count
    row_count = layer_input.shape[2]
    model_width = layer_input.shape[3]
    inner_local = w_zx.shape[3]
    heads_local = w_dt.shape[2]
    bc_local = w_bc.shape[2]
    bc_width = bc_local * shard_count
    inner = inner_local * shard_count
    taps = conv_x.shape[1]
    first_micro = section_index * micro_local

    def mine(array):
        return lax.dynamic_slice_in_dim(array, first_micro, micro_local, 0)[:, 0]

    def sections(value):
        return lax.all_gather(value, "pipe", axis=0)

    input_rows = mine(layer_input)
    cotangent_rows = mine(out_cotangent)
    segment_rows = mine(segment_ids)

    smalls = jnp.concatenate(
        [
            norm_gain[0],
            conv_x[0].reshape(-1),
            conv_x_bias[0],
            gate_gain[0].astype(jnp.float32),
            dt_bias[0],
            a_log[0],
            d_skip[0],
        ]
    )
    smalls_all = sections(smalls)
    bc_taps = jnp.concatenate([conv_bc[0], conv_bc_bias], axis=0).T
    bc_taps_all = lax.all_gather(bc_taps, ("pipe", "tensor"), axis=0, tiled=True)
    bc_taps_all = bc_taps_all.reshape(section_count, bc_width, taps + 1)
    w_bc_all = lax.all_gather(w_bc[0].T, ("pipe", "tensor"), axis=0, tiled=True)
    w_bc_all = w_bc_all.reshape(section_count, bc_width, model_width)
    w_main = jnp.concatenate([w_zx[0, 0].T, w_zx[0, 1].T, w_out[0], w_dt[0].T], axis=0)
    w_main_all = sections(w_main)

    weights = []
    for layer in range(section_count):
        flat = smalls_all[layer]
        parts = []
        start = 0
        for size in (
            model_width,
            taps * inner_local,
            inner_local,
            inner_local,
            heads_local,
            heads_local,
            heads_local,
        ):
            parts.append(flat[start : start + size])
            start += size
        main = w_main_all[layer]
        w_cat = jnp.concatenate(
            [main[: 2 * inner_local], w_bc_all[layer], main[3 * inner_local :]], axis=0
        )
        weights.append(
            dict(
                gain_in=parts[0],
                kernel_x=parts[1].reshape(taps, inner_local),
                offset_x=parts[2],
                gain_out=parts[3],
                step_bias=parts[4],
                decay_log=parts[5],
                skip_gain=parts[6],
                kernel_bc=bc_taps_all[layer, :, :taps].T,
                offset_bc=bc_taps_all[layer, :, taps],
                w_cat=w_cat,
                w_out=main[2 * inner_local : 3 * inner_local],
            )
        )

    def own_rows(values):
        return lax.dynamic_slice_in_dim(values, shard_index * row_count, row_count, 0)

    def forward(hidden_in, segments, layer):
        w = weights[layer]
        hidden = hidden_in.astype(jnp.float32)
        row_scale = lax.rsqrt(jnp.mean(hidden * hidden, axis=-1, keepdims=True) + EPSILON)
        normed = (hidden * row_scale * w["gain_in"]).astype(jnp.bfloat16)
        gathered = lax.all_gather(normed, "tensor", axis=0, tiled=True)
        projected = lax.dot_general(
            gathered, w["w_cat"], (((1,), (1,)), ((), ())), preferred_element_type=jnp.float32
        )
        gate_raw = projected[:, :inner_local]
        x_proj = projected[:, inner_local : 2 * inner_local]
        bc_proj = projected[:, 2 * inner_local : 2 * inner_local + bc_width]
        step_raw = projected[:, 2 * inner_local + bc_width :]
        bc_values, bc_back = jax.vjp(
            lambda values, kernel, offset_bias: bc_activate(values, kernel, offset_bias, segments),
            bc_proj,
            w["kernel_bc"],
            w["offset_bc"],
        )
        bc_values = bc_values.astype(jnp.bfloat16).astype(jnp.float32)
        gated, mix_back = jax.vjp(
            lambda *values: mixer(*values, segments, BLOCK),
            x_proj,
            step_raw,
            bc_values,
            gate_raw,
            w["kernel_x"],
            w["offset_x"],
            w["step_bias"],
            w["decay_log"],
            w["skip_gain"],
        )
        squares = lax.psum(jnp.sum(gated * gated, axis=-1), "tensor")
        gated_scale = lax.rsqrt(squares / inner + EPSILON)[:, None]
        scaled = (gated * w["gain_out"]).astype(jnp.bfloat16)
        partial = jnp.dot(scaled, w["w_out"], preferred_element_type=jnp.float32)
        mixed = lax.psum_scatter(
            partial.astype(jnp.bfloat16), "tensor", scatter_dimension=0, tiled=True
        ).astype(jnp.float32)
        result = (hidden + own_rows(gated_scale) * mixed).astype(jnp.bfloat16)
        kept = (hidden_in, gathered, gated, gated_scale, mixed, bc_back, mix_back)
        return result, kept

    def backward(grad_out, grad_out_all, kept, layer):
        w = weights[layer]
        hidden_in, gathered, gated, gated_scale, mixed, bc_back, mix_back = kept
        own_dots = jnp.sum(grad_out.astype(jnp.float32) * mixed, axis=-1) / inner
        row_dots = lax.all_gather(own_dots, "tensor", axis=0, tiled=True)[:, None]
        out_grad = lax.dot_general(
            grad_out_all, w["w_out"], (((1,), (1,)), ((), ())), preferred_element_type=jnp.float32
        )
        scaled_gated = gated * gated_scale
        normed_out = (scaled_gated * w["gain_out"]).astype(jnp.bfloat16)
        weight_grad = lax.dot_general(
            normed_out, grad_out_all, (((0,), (0,)), ((), ())), preferred_element_type=jnp.float32
        )
        gain_grad = jnp.sum(out_grad * scaled_gated, axis=0)
        gated_grad = gated_scale * (out_grad * w["gain_out"]) - gated * (
            gated_scale**3 * row_dots
        )
        (
            x_grad,
            step_grad,
            bc_grad,
            gate_grad,
            kernel_x_grad,
            offset_x_grad,
            bias_grad,
            decay_grad,
            skip_grad,
        ) = mix_back(gated_grad)
        bc_proj_grad, kernel_bc_grad, offset_bc_grad = bc_back(bc_grad)
        proj_grad = jnp.concatenate([gate_grad, x_grad, bc_proj_grad, step_grad], axis=1).astype(
            jnp.bfloat16
        )
        normed_grad = lax.psum_scatter(
            jnp.dot(proj_grad, w["w_cat"], preferred_element_type=jnp.float32).astype(
                jnp.bfloat16
            ),
            "tensor",
            scatter_dimension=0,
            tiled=True,
        ).astype(jnp.float32)
        cat_grad = lax.dot_general(
            gathered, proj_grad, (((0,), (0,)), ((), ())), preferred_element_type=jnp.float32
        )
        hidden = hidden_in.astype(jnp.float32)
        row_scale = lax.rsqrt(jnp.mean(hidden * hidden, axis=-1, keepdims=True) + EPSILON)
        in_gain_grad = jnp.sum(normed_grad * hidden * row_scale, axis=0)
        scaled_in = normed_grad * w["gain_in"]
        hidden_grad = row_scale * scaled_in - hidden * row_scale**3 * jnp.mean(
            scaled_in * hidden, axis=-1, keepdims=True
        )
        grad_in = (grad_out.astype(jnp.float32) + hidden_grad).astype(jnp.bfloat16)
        local_small = jnp.concatenate(
            [
                kernel_x_grad.reshape(-1),
                offset_x_grad,
                gain_grad,
                bias_grad,
                decay_grad,
                skip_grad,
            ]
        )
        shared_small = jnp.concatenate(
            [kernel_bc_grad.reshape(-1), offset_bc_grad, in_gain_grad]
        )
        return grad_in, (cat_grad, weight_grad, local_small, shared_small)

    micros = range(micro_local)
    grads_flow = [cotangent_rows[micro] for micro in micros]
    flow = [input_rows[micro] for micro in micros]
    kept_all = []
    outputs = []
    for layer in range(section_count):
        results = [forward(flow[micro], segment_rows[micro], layer) for micro in micros]
        flow = [pair[0] for pair in results]
        kept_all.append([pair[1] for pair in results])
        outputs.append(jnp.stack(flow))
    in_grads = [None] * section_count
    totals = [None] * section_count
    for layer in reversed(range(section_count)):
        gathered_grads = [
            lax.all_gather(grads_flow[micro], "tensor", axis=0, tiled=True) for micro in micros
        ]
        results = [
            backward(grads_flow[micro], gathered_grads[micro], kept_all[layer][micro], layer)
            for micro in micros
        ]
        grads_flow = [pair[0] for pair in results]
        in_grads[layer] = jnp.stack(grads_flow)
        summed = results[0][1]
        for pair in results[1:]:
            summed = jax.tree.map(jnp.add, summed, pair[1])
        cat_grad, weight_grad, local_small, shared_small = summed
        bc_first = 2 * inner_local
        bc_sum = lax.psum_scatter(
            cat_grad[:, bc_first : bc_first + bc_width].T.astype(jnp.bfloat16),
            "tensor",
            scatter_dimension=0,
            tiled=True,
        )
        big = (
            cat_grad[:, :bc_first].astype(jnp.bfloat16),
            weight_grad.astype(jnp.bfloat16),
            jnp.concatenate(
                [bc_sum, cat_grad[:, bc_first + bc_width :].T.astype(jnp.bfloat16)], axis=0
            ),
        )
        totals[layer] = (lax.psum(big, ("pipe", "dp")), local_small, shared_small)

    def pick(values):
        chosen = values[0]
        for layer in range(1, section_count):
            chosen = jax.tree.map(
                lambda later, sooner: jnp.where(section_index == layer, later, sooner),
                values[layer],
                chosen,
            )
        return chosen

    def regroup(per_layer):
        stacked = jnp.stack(per_layer)
        moved = lax.all_to_all(stacked, "pipe", split_axis=0, concat_axis=0, tiled=True)
        return moved.reshape((micro_count,) + stacked.shape[2:])

    layer_outputs = regroup(outputs)
    input_grads = regroup(in_grads)
    zx_total, out_total, rest_total = pick([total[0] for total in totals])
    local_total = pick(lax.psum([total[1] for total in totals], ("pipe", "dp")))
    shared_total = pick(lax.psum([total[2] for total in totals], ("pipe", "dp", "tensor")))
    zx_total = zx_total.astype(jnp.float32)
    grad_zx = jnp.stack([zx_total[:, :inner_local], zx_total[:, inner_local:]])[None]
    grad_bc = rest_total[:bc_local].astype(jnp.float32).T[None]
    grad_dt = rest_total[bc_local:].astype(jnp.float32).T[None]
    pieces = []
    start = 0
    for size in (
        taps * inner_local,
        inner_local,
        inner_local,
        heads_local,
        heads_local,
        heads_local,
    ):
        pieces.append(local_total[start : start + size])
        start += size
    kernel_bc_total = shared_total[: taps * bc_width].reshape(taps, bc_width)
    offset_bc_total = shared_total[taps * bc_width : (taps + 1) * bc_width]
    norm_total = shared_total[(taps + 1) * bc_width :]
    return (
        layer_outputs[None, :, None],
        input_grads[None, :, None],
        norm_total[None],
        grad_zx,
        grad_bc,
        grad_dt,
        pieces[0].reshape(1, taps, inner_local),
        pieces[1][None],
        lax.dynamic_slice_in_dim(kernel_bc_total, shard_index * bc_local, bc_local, 1)[None],
        lax.dynamic_slice_in_dim(offset_bc_total, shard_index * bc_local, bc_local, 0)[None],
        pieces[3][None],
        pieces[4][None],
        pieces[5][None],
        pieces[2][None],
        out_total.astype(jnp.float32)[None],
    )


def solution(mesh):
    return jax.shard_map(
        local,
        mesh=mesh,
        in_specs=(
            P(None, "dp", "tensor", None),
            P(None, "dp", None),
            P(None, "dp", "tensor", None),
            P("pipe", None),
            P("pipe", None, None, "tensor"),
            P("pipe", None, "tensor"),
            P("pipe", None, "tensor"),
            P("pipe", None, "tensor"),
            P("pipe", "tensor"),
            P("pipe", None, "tensor"),
            P("pipe", "tensor"),
            P("pipe", "tensor"),
            P("pipe", "tensor"),
            P("pipe", "tensor"),
            P("pipe", "tensor"),
            P("pipe", "tensor", None),
        ),
        out_specs=(
            P("pipe", None, "dp", "tensor", None),
            P("pipe", None, "dp", "tensor", None),
            P("pipe", None),
            P("pipe", None, None, "tensor"),
            P("pipe", None, "tensor"),
            P("pipe", None, "tensor"),
            P("pipe", None, "tensor"),
            P("pipe", "tensor"),
            P("pipe", None, "tensor"),
            P("pipe", "tensor"),
            P("pipe", "tensor"),
            P("pipe", "tensor"),
            P("pipe", "tensor"),
            P("pipe", "tensor"),
            P("pipe", "tensor", None),
        ),
        check_vma=False,
    )
```

time: 1850 us -> 1120 us (0.61)
  other arithmetic: 436 us -> 132 us
  matrix products: 399 us -> 197 us
  local copies, waits for them, and re-layouts: 277 us -> 137 us
  starting transfers between devices: 67.1 us -> 20 us
  waiting for transfers between devices: 493 us -> 449 us
  loops' own time: 33.3 us -> 0 us
  blocking collectives: 123 us -> 154 us
    another operation x61 -> x15, other arithmetic: 168 us -> 14.1 us
    all_to_all x10 -> x2, waiting for transfers between devices: 120 us -> 11.1 us  [regroup(): lax.all_to_all(stacked, 'pipe', split_axis=0, concat_axis=0, tiled=True)]
    dot_general x50 -> x44, matrix products: 200 us -> 107 us  [the longest x4 23.4 us: backward(): lax.dot_general(grad_out_all, w['w_out'], (((1,), (1,)), ((), ())), prefe...]
    select_n x40 -> x3, other arithmetic: 83.6 us -> 0.02 us  [pick(): jnp.where(section_index == layer, later, sooner)]
    dot_general x20 -> x12, matrix products: 125 us -> 52.6 us  [state_scan(): jnp.einsum('chts,cshp->cthp', affinity[:, None] * decays, weighted, preci...]
    psum x2 -> x4, blocking collectives: 21.9 us -> 85.8 us  [the longest x1 38.3 us: local(): lax.psum([total[2] for total in totals], ('pipe', 'dp', 'tensor'))]
    all_gather x1 -> x6, waiting for transfers between devices: 31.3 us -> 93.4 us  [the longest x4 54.4 us: local(): lax.all_gather(grads_flow[micro], 'tensor', axis=0, tiled=True)]
    dynamic_slice x40 -> x0, local copies, waits for them, and re-layouts: 48.6 us -> none  [pick_row(): return lax.dynamic_index_in_dim(buffer, micro_index, 0, keepdims=False)]
  transfers between devices with their start and end apart: 38 -> 23, of which waited for: 33 -> 18; matrix products, arithmetic and copies ran while one was open for 21% -> 19% of each run, Pallas kernels for 0% -> 0%
where the time goes in v1:
time: 1120 us; the launch traced here: 1110 us
  waiting for transfers between devices  449 us (40%)
  matrix products  197 us (18%)
  blocking collectives  154 us (14%)
  local copies, waits for them, and re-layouts  137 us (12%)
  other arithmetic  132 us (12%)
  between operations  21.8 us (2%)
  starting transfers between devices  20 us (2%)
    reduce_scatter x4, waiting for transfers between devices, forward(): lax.psum_scatter(partial.astype(jnp.bfloat16), 'tensor', scatter_dimensio...  104 us
    reduce_scatter x4, waiting for transfers between devices, backward(): lax.psum_scatter(jnp.dot(proj_grad, w['w_cat'], preferred_element_type=jn...  98.9 us
    all_gather x4, waiting for transfers between devices, forward(): gathered = lax.all_gather(normed, 'tensor', axis=0, tiled=True)  89.9 us
    all_gather x4, waiting for transfers between devices, local(): lax.all_gather(grads_flow[micro], 'tensor', axis=0, tiled=True)  54.4 us
    dot_general x12, matrix products, state_scan(): jnp.einsum('chts,cshp->cthp', affinity[:, None] * decays, weighted, preci...  52.6 us
    psum x1, waiting for transfers between devices, local(): totals[layer] = (lax.psum(big, ('pipe', 'dp')), local_small, shared_small)  48.3 us
    all_gather x1, waiting for transfers between devices, sections(): return lax.all_gather(value, 'pipe', axis=0)  39.1 us
    psum x1, blocking collectives, local(): lax.psum([total[2] for total in totals], ('pipe', 'dp', 'tensor'))  38.3 us
  transfers between devices with their start and end apart: 23, of which 18 were waited for; matrix products, arithmetic and copies ran while one was open for 19% of the time, Pallas kernels for 0%

profile of v1, /device:TPU:0, one launch (start us, length us, event | category | flops | bytes accessed | tf_op | source)
XLA Modules:
  0.0 1111.1 jit_solution(12739664903824641716)
XLA Ops:
  12.9 9.8 all-reduce.110
  28.4 21.0 %all-gather.5 = f32[16,32,5]{1,2,0:T(8,128)S(1)} all-gather(f32[1,32,5]{1,2,0:T(8,128)S(1)} %maximum_bitcast_fusion.6), channel_id=1, replica_groups=mesh['pipe'=2,'dp'=2,'tensor'=8] {'pipe','tensor'}, dimensions={0}, use_global_device_ids=true | all-gather | bytes 10880 | tf_op jit(solution)/shard_map/all_gather | solution.py:165
  58.3 39.1 %all-gather.39.cloned.1.call-done = bf16[2,772,1024]{2,1,0:T(8,128)(2,1)} async-done(((bf16[1,772,1024]{2,1,0:T(8,128)(2,1)}), bf16[2,772,1024]{2,1,0:T(8,128)(2,1)}) %all-gather.39.cloned.1.call-update) | async-done | bytes 3162128 | tf_op jit(solution)/shard_map/all_gather | solution.py:146
  101.7 26.4 %all-gather.25.cloned.1.call-done = bf16[1024,1024]{1,0:T(8,128)(2,1)} async-done(((bf16[128,1024]{1,0:T(8,128)(2,1)}), bf16[1024,1024]{1,0:T(8,128)(2,1)}) %all-gather.25.cloned.1.call-update) | async-done | bytes 2097168 | tf_op jit(solution)/shard_map/all_gather | solution.py:216
  128.1 3.8 fusion.553
  133.6 24.6 %all-gather.21.cloned.1.call-done = bf16[1024,1024]{1,0:T(8,128)(2,1)} async-done(((bf16[128,1024]{1,0:T(8,128)(2,1)}), bf16[1024,1024]{1,0:T(8,128)(2,1)}) %all-gather.21.cloned.1.call-update) | async-done | bytes 2097168 | tf_op jit(solution)/shard_map/all_gather | solution.py:216
  158.2 3.9 fusion.554
  173.2 7.4 fusion.200
  220.9 16.0 %all-reduce.113 = (f32[1024]{0:T(1024)S(1)}, f32[1024]{0:T(1024)S(1)}) all-reduce(f32[1024]{0:T(1024)S(1)} %get-tuple-element.526, f32[1024]{0:T(1024)S(1)} %get-tuple-element.271), channel_id=1, replica_groups=mesh['pipe'=2,'dp'=2,'tensor'=8] {'tensor'}, use_global_device_ids=true, to_apply=%region_6.8 | all-reduce | flops 2048 | bytes 16384 | tf_op jit(solution)/shard_map/psum | solution.py:243
  237.1 16.3 %reduce-scatter.11.cloned.1.call-done = bf16[128,1024]{1,0:T(8,128)(2,1)} async-done(((bf16[1024,1024]{1,0:T(8,128)(2,1)}), bf16[128,1024]{1,0:T(8,128)(2,1)}) %reduce-scatter.11.cloned.1.call-update) | async-done | bytes 262160 | tf_op jit(solution)/shard_map/reduce_scatter | solution.py:247
  253.4 37.1 %reduce-scatter.13.cloned.1.call-done = bf16[128,1024]{1,0:T(8,128)(2,1)} async-done(((bf16[1024,1024]{1,0:T(8,128)(2,1)}), bf16[128,1024]{1,0:T(8,128)(2,1)}) %reduce-scatter.13.cloned.1.call-update) | async-done | bytes 262160 | tf_op jit(solution)/shard_map/reduce_scatter | solution.py:247
  295.6 10.7 reduce-scatter.15.cloned.1.call-start
  307.6 15.0 %all-gather.29.cloned.1.call-done = bf16[1024,1024]{1,0:T(8,128)(2,1)} async-done(((bf16[128,1024]{1,0:T(8,128)(2,1)}), bf16[1024,1024]{1,0:T(8,128)(2,1)}) %all-gather.29.cloned.1.call-update) | async-done | bytes 2097168 | tf_op jit(solution)/shard_map/all_gather | solution.py:216
  329.6 23.8 %all-gather.27.cloned.1.call-done = bf16[1024,1024]{1,0:T(8,128)(2,1)} async-done(((bf16[128,1024]{1,0:T(8,128)(2,1)}), bf16[1024,1024]{1,0:T(8,128)(2,1)}) %all-gather.27.cloned.1.call-update) | async-done | bytes 2097168 | tf_op jit(solution)/shard_map/all_gather | solution.py:216
  372.1 7.0 fusion.196
  405.2 3.8 fusion.118
  410.2 4.4 multiply_reduce_fusion.57
  422.6 16.5 %all-reduce.112 = (f32[1024]{0:T(1024)}, f32[1024]{0:T(1024)}) all-reduce(f32[1024]{0:T(1024)} %get-tuple-element.522, f32[1024]{0:T(1024)} %get-tuple-element.245), channel_id=1, replica_groups=mesh['pipe'=2,'dp'=2,'tensor'=8] {'tensor'}, use_global_device_ids=true, to_apply=%region_14.16 | all-reduce | flops 2048 | bytes 16384 | tf_op jit(solution)/shard_map/psum | solution.py:243
  441.0 13.4 %reduce-scatter.15.cloned.1.call-done = bf16[128,1024]{1,0:T(8,128)(2,1)} async-done(((bf16[1024,1024]{1,0:T(8,128)(2,1)}), bf16[128,1024]{1,0:T(8,128)(2,1)}) %reduce-scatter.15.cloned.1.call-update) | async-done | bytes 262160 | tf_op jit(solution)/shard_map/reduce_scatter | solution.py:247
  454.4 37.0 %reduce-scatter.17.cloned.1.call-done = bf16[128,1024]{1,0:T(8,128)(2,1)} async-done(((bf16[1024,1024]{1,0:T(8,128)(2,1)}), bf16[128,1024]{1,0:T(8,128)(2,1)}) %reduce-scatter.17.cloned.1.call-update) | async-done | bytes 262160 | tf_op jit(solution)/shard_map/reduce_scatter | solution.py:247
  495.5 8.4 all-gather.8
  504.5 10.4 all-gather.6
  517.5 4.7 all-gather.35.cloned.1.call-done
  525.6 26.7 %all-gather.37.cloned.1.call-done = bf16[1,1,1024,1024]{3,2,1,0:T(8,128)(2,1)} async-done(((bf16[1,1,128,1024]{3,2,1,0:T(8,128)(2,1)}), bf16[1,1,1024,1024]{3,2,1,0:T(8,128)(2,1)}) %all-gather.37.cloned.1.call-update) | async-done | bytes 2097168 | tf_op jit(solution)/shard_map/all_gather | solution.py:334
  552.3 8.6 multiply_reduce_fusion.16
  575.0 6.1 fusion.29
  595.3 5.8 fusion.25
  619.5 4.5 fusion.121
  648.4 4.1 multiply_multiply_fusion.20
  655.3 3.8 convolution_convert_fusion.7
  669.3 25.1 %reduce-scatter.19.cloned.1.call-done = bf16[128,1024]{1,0:T(8,128)(2,1)} async-done(((bf16[1024,1024]{1,0:T(8,128)(2,1)}), bf16[128,1024]{1,0:T(8,128)(2,1)}) %reduce-scatter.19.cloned.1.call-update) | async-done | bytes 262160 | tf_op jit(solution)/shard_map/reduce_scatter | solution.py:286
  694.5 36.7 %reduce-scatter.23.cloned.1.call-done = bf16[128,1024]{1,0:T(8,128)(2,1)} async-done(((bf16[1024,1024]{1,0:T(8,128)(2,1)}), bf16[128,1024]{1,0:T(8,128)(2,1)}) %reduce-scatter.23.cloned.1.call-update) | async-done | bytes 262160 | tf_op jit(solution)/shard_map/reduce_scatter | solution.py:286
  737.3 4.0 fusion.343
  746.8 8.5 all-gather.9
  756.6 10.3 all-gather.7
  771.5 23.0 %all-gather.33.cloned.1.call-done = bf16[1024,1024]{1,0:T(8,128)(2,1)} async-done(((bf16[128,1024]{1,0:T(8,128)(2,1)}), bf16[1024,1024]{1,0:T(8,128)(2,1)}) %all-gather.33.cloned.1.call-update) | async-done | bytes 2097168 | tf_op jit(solution)/shard_map/all_gather | solution.py:334
  794.5 8.1 multiply_reduce_fusion.4
  815.2 6.1 fusion.31
  834.3 5.9 fusion.27
  892.7 5.1 convolution_convert_fusion.6
  898.1 4.9 convolution_convert_fusion.4
  913.0 3.7 all-to-all-start
  919.9 11.1 all-to-all-done
  942.9 15.0 %all-reduce.114 = (f32[1548]{0:T(1024)S(1)}, f32[1548]{0:T(1024)S(1)}) all-reduce(f32[1548]{0:T(1024)S(1)} %add.813, f32[1548]{0:T(1024)S(1)} %add.814), channel_id=1, replica_groups=mesh['pipe'=2,'dp'=2,'tensor'=8] {'pipe','dp'}, use_global_device_ids=true, to_apply=%region_120.122 | all-reduce | flops 3096 | bytes 24768 | tf_op jit(solution)/shard_map/psum | solution.py:380
  960.1 36.7 %reduce-scatter.25.cloned.1.call-done = bf16[128,1024]{1,0:T(8,128)(2,1)} async-done(((bf16[1024,1024]{1,0:T(8,128)(2,1)}), bf16[128,1024]{1,0:T(8,128)(2,1)}) %reduce-scatter.25.cloned.1.call-update) | async-done | bytes 262160 | tf_op jit(solution)/shard_map/reduce_scatter | solution.py:286
  998.2 38.3 %all-reduce.111 = (f32[2304]{0:T(1024)S(1)}, f32[2304]{0:T(1024)S(1)}) all-reduce(f32[2304]{0:T(1024)S(1)} %maximum_add_fusion, f32[2304]{0:T(1024)S(1)} %maximum_add_fusion.1), channel_id=1, replica_groups=mesh['pipe'=2,'dp'=2,'tensor'=8] {'pipe','dp','tensor'}, use_global_device_ids=true, to_apply=%region_80.82 | all-reduce | flops 4608 | bytes 36864 | tf_op jit(solution)/shard_map/psum | solution.py:381
  1039.7 4.4 all-to-all-start.1
  1045.4 48.3 %all-reduce.118.cloned.1.call-done = (bf16[1024,512]{0,1:T(8,128)(2,1)}, bf16[1024,512]{0,1:T(8,128)(2,1)}, bf16[36,1024]{1,0:T(8,128)(2,1)}, bf16[36,1024]{1,0:...) async-done(((bf16[1024,512]{0,1:T(8,128)(2,1)}, bf16[1024,512]{0,1:T(8,128)(2,1)}, bf16[36,1024]{1,0:T(8,128)(2,1)}, bf16[36,1024]{1,0:T(8,128)(2,1)}, ...) | async-done | bytes 3293200 | tf_op jit(solution)/shard_map/psum | solution.py:360
  (1380 shorter events, 374.0 us)
Async XLA Ops:
  7.2 48.9 %all-gather.23.cloned.1.call-start = ((), (), s32[]{:S(2)}) async-start(), calls=%async_computation.13 | async-start | bytes 1114112 | tf_op jit(solution)/shard_map/all_gather | solution.py:167
  7.9 89.4 %all-gather.39.cloned.1.call-start = ((), (), s32[]{:S(2)}) async-start(), calls=%async_computation.31 | async-start | bytes 4767744 | tf_op jit(solution)/shard_map/all_gather | solution.py:146
  11.2 117.0 %all-gather.25.cloned.1.call-start = ((), (), s32[]{:S(2)}) async-start(), calls=%async_computation.15 | async-start | bytes 2359296 | tf_op jit(solution)/shard_map/all_gather | solution.py:216
  25.3 132.9 %all-gather.21.cloned.1.call-start = ((), (), s32[]{:S(2)}) async-start(), calls=%async_computation.12 | async-start | bytes 2359296 | tf_op jit(solution)/shard_map/all_gather | solution.py:216
  25.9 227.5 %reduce-scatter.11.cloned.1.call-start = ((), (), s32[]{:S(2)}) async-start(), calls=%async_computation.14 | async-start | bytes 2359296 | tf_op jit(solution)/shard_map/reduce_scatter | solution.py:247
  28.0 134.3 %copy-start.394 = (f32[4]{0:T(128)}, f32[4]{0:T(128)S(1)}, u32[]{:S(2)}) copy-start(f32[4]{0:T(128)S(1)} %get-tuple-element.405) | copy-start | bytes 52
  28.0 134.3 %copy-start.396 = (f32[4]{0:T(128)}, f32[4]{0:T(128)S(1)}, u32[]{:S(2)}) copy-start(f32[4]{0:T(128)S(1)} %get-tuple-element.406) | copy-start | bytes 52
  50.1 114.9 %copy-start.361 = (f32[1,256,1]{1,0,2:T(1,128)}, f32[1,256,1]{1,0,2:T(1,128)S(1)}, u32[]{:S(2)}) copy-start(f32[1,256,1]{1,0,2:T(1,128)S(1)} %get-tuple-element.446) | copy-start | bytes 3076
  50.2 113.3 %copy-start.351 = (f32[4]{0:T(128)}, f32[4]{0:T(128)S(1)}, u32[]{:S(2)}) copy-start(f32[4]{0:T(128)S(1)} %get-tuple-element.552) | copy-start | bytes 52
  50.2 114.2 %copy-start.354 = (f32[4]{0:T(128)}, f32[4]{0:T(128)S(1)}, u32[]{:S(2)}) copy-start(f32[4]{0:T(128)S(1)} %get-tuple-element.553) | copy-start | bytes 52
  52.1 121.0 %copy-start.327 = (f32[1,256]{1,0:T(1,128)}, f32[1,256]{1,0:T(1,128)S(1)}, u32[]{:S(2)}) copy-start(f32[1,256]{1,0:T(1,128)S(1)} %get-tuple-element.489) | copy-start | bytes 3076
  52.1 121.0 %copy-start.329 = (f32[1,256]{1,0:T(1,128)}, f32[1,256]{1,0:T(1,128)S(1)}, u32[]{:S(2)}) copy-start(f32[1,256]{1,0:T(1,128)S(1)} %get-tuple-element.490) | copy-start | bytes 3076
  52.2 121.0 %copy-start.331 = (f32[1,256]{1,0:T(1,128)}, f32[1,256]{1,0:T(1,128)S(1)}, u32[]{:S(2)}) copy-start(f32[1,256]{1,0:T(1,128)S(1)} %get-tuple-element.491) | copy-start | bytes 3076
  52.2 121.0 %copy-start.333 = (f32[1,256]{1,0:T(1,128)}, f32[1,256]{1,0:T(1,128)S(1)}, u32[]{:S(2)}) copy-start(f32[1,256]{1,0:T(1,128)S(1)} %get-tuple-element.492) | copy-start | bytes 3076
  52.2 142.3 %copy-start.263 = (f32[4,256]{1,0:T(4,128)}, f32[4,256]{1,0:T(4,128)S(1)}, u32[]{:S(2)}) copy-start(f32[4,256]{1,0:T(4,128)S(1)} %get-tuple-element.488) | copy-start | bytes 12292
  52.2 142.3 %copy-start.297 = (f32[4,256]{1,0:T(4,128)}, f32[4,256]{1,0:T(4,128)S(1)}, u32[]{:S(2)}) copy-start(f32[4,256]{1,0:T(4,128)S(1)} %get-tuple-element.487) | copy-start | bytes 12292
  52.3 142.1 %copy-start.259 = (f32[4,256]{1,0:T(4,128)}, f32[4,256]{1,0:T(4,128)S(1)}, u32[]{:S(2)}) copy-start(f32[4,256]{1,0:T(4,128)S(1)} %get-tuple-element.483) | copy-start | bytes 12292
  52.3 142.1 %copy-start.293 = (f32[4,256]{1,0:T(4,128)}, f32[4,256]{1,0:T(4,128)S(1)}, u32[]{:S(2)}) copy-start(f32[4,256]{1,0:T(4,128)S(1)} %get-tuple-element.482) | copy-start | bytes 12292
  52.9 112.1 %copy-start.358 = (f32[1,256]{1,0:T(1,128)}, f32[1,256]{1,0:T(1,128)S(1)}, u32[]{:S(2)}) copy-start(f32[1,256]{1,0:T(1,128)S(1)} %get-tuple-element.400) | copy-start | bytes 3076
  52.9 120.2 %copy-start.309 = (f32[1,256]{1,0:T(1,128)}, f32[1,256]{1,0:T(1,128)S(1)}, u32[]{:S(2)}) copy-start(f32[1,256]{1,0:T(1,128)S(1)} %get-tuple-element.396) | copy-start | bytes 3076
  52.9 120.2 %copy-start.311 = (f32[1,256]{1,0:T(1,128)}, f32[1,256]{1,0:T(1,128)S(1)}, u32[]{:S(2)}) copy-start(f32[1,256]{1,0:T(1,128)S(1)} %get-tuple-element.397) | copy-start | bytes 3076
  53.0 120.2 %copy-start.313 = (f32[1,256]{1,0:T(1,128)}, f32[1,256]{1,0:T(1,128)S(1)}, u32[]{:S(2)}) copy-start(f32[1,256]{1,0:T(1,128)S(1)} %get-tuple-element.398) | copy-start | bytes 3076
  53.0 120.2 %copy-start.315 = (f32[1,256]{1,0:T(1,128)}, f32[1,256]{1,0:T(1,128)S(1)}, u32[]{:S(2)}) copy-start(f32[1,256]{1,0:T(1,128)S(1)} %get-tuple-element.399) | copy-start | bytes 3076
  53.0 112.0 %copy-start.211 = (f32[1024]{0:T(1024)}, f32[1024]{0:T(1024)S(1)}, u32[]{:S(2)}) copy-start(f32[1024]{0:T(1024)S(1)} %get-tuple-element.558) | copy-start | bytes 12292
  53.1 112.0 %copy-start.215 = (f32[1024]{0:T(1024)}, f32[1024]{0:T(1024)S(1)}, u32[]{:S(2)}) copy-start(f32[1024]{0:T(1024)S(1)} %get-tuple-element.559) | copy-start | bytes 12292
  53.1 112.0 %copy-start.219 = (f32[1024]{0:T(1024)}, f32[1024]{0:T(1024)S(1)}, u32[]{:S(2)}) copy-start(f32[1024]{0:T(1024)S(1)} %get-tuple-element.560) | copy-start | bytes 12292
  53.1 120.1 %copy-start.202 = (f32[1024]{0:T(1024)}, f32[1024]{0:T(1024)S(1)}, u32[]{:S(2)}) copy-start(f32[1024]{0:T(1024)S(1)} %get-tuple-element.493) | copy-start | bytes 12292
  53.1 120.1 %copy-start.205 = (f32[1024]{0:T(1024)}, f32[1024]{0:T(1024)S(1)}, u32[]{:S(2)}) copy-start(f32[1024]{0:T(1024)S(1)} %get-tuple-element.494) | copy-start | bytes 12292
  53.1 120.1 %copy-start.208 = (f32[1024]{0:T(1024)}, f32[1024]{0:T(1024)S(1)}, u32[]{:S(2)}) copy-start(f32[1024]{0:T(1024)S(1)} %get-tuple-element.495) | copy-start | bytes 12292
  217.6 72.9 %reduce-scatter.13.cloned.1.call-start = ((), (), s32[]{:S(2)}) async-start(), calls=%async_computation.16 | async-start | bytes 2359296 | tf_op jit(solution)/shard_map/reduce_scatter | solution.py:247
  220.8 101.9 %copy-start.187 = (bf16[256,1024]{1,0:T(8,128)(2,1)S(1)}, bf16[256,1024]{1,0:T(8,128)(2,1)}, u32[]{:S(2)}) copy-start(bf16[256,1024]{1,0:T(8,128)(2,1)} %get-tuple-element.359) | copy-start | bytes 1572868
  220.8 101.8 %all-gather.29.cloned.1.call-start = ((), (), s32[]{:S(2)}) async-start(), calls=%async_computation.19 | async-start | bytes 2359296 | tf_op jit(solution)/shard_map/all_gather | solution.py:216
  294.8 58.6 %all-gather.27.cloned.1.call-start = ((), (), s32[]{:S(2)}) async-start(), calls=%async_computation.17 | async-start | bytes 2359296 | tf_op jit(solution)/shard_map/all_gather | solution.py:216
  295.6 158.8 %reduce-scatter.15.cloned.1.call-start = ((), (), s32[]{:S(2)}) async-start(), calls=%async_computation.18 | async-start | bytes 2359296 | tf_op jit(solution)/shard_map/reduce_scatter | solution.py:247
  418.9 72.5 %reduce-scatter.17.cloned.1.call-start = ((), (), s32[]{:S(2)}) async-start(), calls=%async_computation.20 | async-start | bytes 2359296 | tf_op jit(solution)/shard_map/reduce_scatter | solution.py:247
  422.6 99.6 %all-gather.35.cloned.1.call-start = ((), (), s32[]{:S(2)}) async-start(), calls=%async_computation.29 | async-start | bytes 2359296 | tf_op jit(solution)/shard_map/all_gather | solution.py:334
  494.2 58.1 %all-gather.37.cloned.1.call-start = ((), (), s32[]{:S(2)}) async-start(), calls=%async_computation.30 | async-start | bytes 2359296 | tf_op jit(solution)/shard_map/all_gather | solution.py:334
  494.8 199.7 %reduce-scatter.19.cloned.1.call-start = ((), (), s32[]{:S(2)}) async-start(), calls=%async_computation.21 | async-start | bytes 2359296 | tf_op jit(solution)/shard_map/reduce_scatter | solution.py:286
  659.1 72.1 %reduce-scatter.23.cloned.1.call-start = ((), (), s32[]{:S(2)}) async-start(), calls=%async_computation.24 | async-start | bytes 2359296 | tf_op jit(solution)/shard_map/reduce_scatter | solution.py:286
  668.0 100.2 %all-gather.31.cloned.1.call-start = ((), (), s32[]{:S(2)}) async-start(), calls=%async_computation.22 | async-start | bytes 2359296 | tf_op jit(solution)/shard_map/all_gather | solution.py:334
  736.4 58.1 %all-gather.33.cloned.1.call-start = ((), (), s32[]{:S(2)}) async-start(), calls=%async_computation.25 | async-start | bytes 2359296 | tf_op jit(solution)/shard_map/all_gather | solution.py:334
  737.0 180.5 %reduce-scatter.27.cloned.1.call-start = ((), (), s32[]{:S(2)}) async-start(), calls=%async_computation.27 | async-start | bytes 589824 | tf_op jit(solution)/shard_map/reduce_scatter | solution.py:347
  745.4 194.5 %reduce-scatter.29.cloned.1.call-start = ((), (), s32[]{:S(2)}) async-start(), calls=%async_computation.28 | async-start | bytes 589824 | tf_op jit(solution)/shard_map/reduce_scatter | solution.py:347
  892.7 67.5 %reduce-scatter.21.cloned.1.call-start = ((), (), s32[]{:S(2)}) async-start(), calls=%async_computation.23 | async-start | bytes 2359296 | tf_op jit(solution)/shard_map/reduce_scatter | solution.py:286
  897.8 99.0 %reduce-scatter.25.cloned.1.call-start = ((), (), s32[]{:S(2)}) async-start(), calls=%async_computation.26 | async-start | bytes 2359296 | tf_op jit(solution)/shard_map/reduce_scatter | solution.py:286
  913.0 18.0 %all-to-all-start = ((bf16[2,2,128,1024]{3,2,1,0:T(8,128)(2,1)}), bf16[2,2,128,1024]{3,2,1,0:T(8,128)(2,1)S(1)}, u32[]{:S(2)}, u32[]{:S(2)}) async-start(bf16[2,2,128,1024]{3,2,1,0:T(8,128)(2,1)} %pad_maximum_fusion.6), calls=%async_computation.4 | async-start | bytes 2097152 | tf_op jit(solution)/shard_map/all_to_all | solution.py:374
  916.7 177.0 %all-reduce.118.cloned.1.call-start = ((), (), s32[]{:S(2)}) async-start(), calls=%async_computation.32 | async-start | bytes 6619136 | tf_op jit(solution)/shard_map/psum | solution.py:360
  1039.7 61.0 %all-to-all-start.1 = ((bf16[2,2,128,1024]{3,2,1,0:T(8,128)(2,1)}), bf16[2,2,128,1024]{3,2,1,0:T(8,128)(2,1)}, u32[]{:S(2)}, u32[]{:S(2)}) async-start(bf16[2,2,128,1024]{3,2,1,0:T(8,128)(2,1)} %pad_maximum_fusion.7), calls=%async_computation.9 | async-start | bytes 2097152 | tf_op jit(solution)/shard_map/all_to_all | solution.py:374
  (467 other events, 3612.5 us)
Sparse Core Ops, SparseCore 0:
  10.2 40.5 all-gather.22
  53.0 44.3 all-gather.38
  99.0 29.0 all-gather.24
  129.6 28.5 all-gather.20
  217.7 35.5 reduce-scatter.10
  255.5 34.9 reduce-scatter.12
  295.0 27.6 all-gather.28
  324.9 28.5 all-gather.26
  419.0 35.3 reduce-scatter.14
  456.5 34.8 reduce-scatter.16
  494.3 27.8 all-gather.34
  523.6 28.5 all-gather.36
  659.2 35.2 reduce-scatter.18
  696.6 34.4 reduce-scatter.22
  736.5 27.8 all-gather.30
  765.9 28.5 all-gather.32
  796.6 30.4 reduce-scatter.26
  892.8 30.4 reduce-scatter.28
  926.2 33.9 reduce-scatter.20
  962.3 34.4 reduce-scatter.24
  1001.8 91.8 all-reduce.117

commit v2 on v1

--- a/solution.py
+++ b/solution.py
@@ -161,13 +161,22 @@
         ]
     )
     smalls_all = sections(smalls)
-    bc_taps = jnp.concatenate([conv_bc[0], conv_bc_bias], axis=0).T
-    bc_taps_all = lax.all_gather(bc_taps, ("pipe", "tensor"), axis=0, tiled=True)
-    bc_taps_all = bc_taps_all.reshape(section_count, bc_width, taps + 1)
-    w_bc_all = lax.all_gather(w_bc[0].T, ("pipe", "tensor"), axis=0, tiled=True)
-    w_bc_all = w_bc_all.reshape(section_count, bc_width, model_width)
-    w_main = jnp.concatenate([w_zx[0, 0].T, w_zx[0, 1].T, w_out[0], w_dt[0].T], axis=0)
+    left = jnp.concatenate([conv_bc[0], conv_bc_bias], axis=0).T
+    terms = []
+    for _ in range(3):
+        term = lax.reduce_precision(left, 8, 7)
+        terms.append(term.astype(jnp.bfloat16))
+        left = left - term
+    filler = jnp.zeros((bc_local, 128 - 3 * (taps + 1)), jnp.bfloat16)
+    bc_pack = jnp.concatenate([w_bc[0].T] + terms + [filler], axis=1)
+    bc_all = lax.all_gather(bc_pack, ("pipe", "tensor"), axis=0, tiled=True)
+    bc_all = bc_all.reshape(section_count, bc_width, model_width + 128)
+    w_bc_all = bc_all[:, :, :model_width]
+    taps_terms = bc_all[:, :, model_width : model_width + 3 * (taps + 1)].astype(jnp.float32)
+    bc_taps_all = jnp.sum(taps_terms.reshape(section_count, bc_width, 3, taps + 1), axis=2)
+    w_main = jnp.concatenate([w_zx[0, 0].T, w_zx[0, 1].T, w_dt[0].T], axis=0)
     w_main_all = sections(w_main)
+    w_out_all = sections(w_out[0])
 
     weights = []
     for layer in range(section_count):
@@ -187,7 +196,7 @@
             start += size
         main = w_main_all[layer]
         w_cat = jnp.concatenate(
-            [main[: 2 * inner_local], w_bc_all[layer], main[3 * inner_local :]], axis=0
+            [main[: 2 * inner_local], w_bc_all[layer], main[2 * inner_local :]], axis=0
         )
         weights.append(
             dict(
@@ -201,14 +210,14 @@
                 kernel_bc=bc_taps_all[layer, :, :taps].T,
                 offset_bc=bc_taps_all[layer, :, taps],
                 w_cat=w_cat,
-                w_out=main[2 * inner_local : 3 * inner_local],
+                w_out=w_out_all[layer],
             )
         )
 
     def own_rows(values):
         return lax.dynamic_slice_in_dim(values, shard_index * row_count, row_count, 0)
 
-    def forward(hidden_in, segments, layer):
+    def forward(hidden_in, segments, layer, order):
         w = weights[layer]
         hidden = hidden_in.astype(jnp.float32)
         row_scale = lax.rsqrt(jnp.mean(hidden * hidden, axis=-1, keepdims=True) + EPSILON)
@@ -224,7 +233,7 @@
         bc_values, bc_back = jax.vjp(
             lambda values, kernel, offset_bias: bc_activate(values, kernel, offset_bias, segments),
             bc_proj,
-            w["kernel_bc"],
+            w["kernel_bc"] + order,
             w["offset_bc"],
         )
         bc_values = bc_values.astype(jnp.bfloat16).astype(jnp.float32)
@@ -234,7 +243,7 @@
             step_raw,
             bc_values,
             gate_raw,
-            w["kernel_x"],
+            w["kernel_x"] + order,
             w["offset_x"],
             w["step_bias"],
             w["decay_log"],
@@ -249,13 +258,11 @@
         ).astype(jnp.float32)
         result = (hidden + own_rows(gated_scale) * mixed).astype(jnp.bfloat16)
         kept = (hidden_in, gathered, gated, gated_scale, mixed, bc_back, mix_back)
-        return result, kept
-
-    def backward(grad_out, grad_out_all, kept, layer):
+        return result, kept, 0.0 * (partial[0, 0] + squares[0])
+
+    def backward(grad_out, grad_out_all, row_dots, kept, layer, order):
         w = weights[layer]
         hidden_in, gathered, gated, gated_scale, mixed, bc_back, mix_back = kept
-        own_dots = jnp.sum(grad_out.astype(jnp.float32) * mixed, axis=-1) / inner
-        row_dots = lax.all_gather(own_dots, "tensor", axis=0, tiled=True)[:, None]
         out_grad = lax.dot_general(
             grad_out_all, w["w_out"], (((1,), (1,)), ((), ())), preferred_element_type=jnp.float32
         )
@@ -265,7 +272,7 @@
             normed_out, grad_out_all, (((0,), (0,)), ((), ())), preferred_element_type=jnp.float32
         )
         gain_grad = jnp.sum(out_grad * scaled_gated, axis=0)
-        gated_grad = gated_scale * (out_grad * w["gain_out"]) - gated * (
+        gated_grad = gated_scale * (out_grad * (w["gain_out"] + order)) - gated * (
             gated_scale**3 * row_dots
         )
         (
@@ -283,10 +290,9 @@
         proj_grad = jnp.concatenate([gate_grad, x_grad, bc_proj_grad, step_grad], axis=1).astype(
             jnp.bfloat16
         )
+        spread_grad = jnp.dot(proj_grad, w["w_cat"], preferred_element_type=jnp.float32)
         normed_grad = lax.psum_scatter(
-            jnp.dot(proj_grad, w["w_cat"], preferred_element_type=jnp.float32).astype(
-                jnp.bfloat16
-            ),
+            spread_grad.astype(jnp.bfloat16),
             "tensor",
             scatter_dimension=0,
             tiled=True,
@@ -315,15 +321,23 @@
         shared_small = jnp.concatenate(
             [kernel_bc_grad.reshape(-1), offset_bc_grad, in_gain_grad]
         )
-        return grad_in, (cat_grad, weight_grad, local_small, shared_small)
+        order = 0.0 * spread_grad[0, 0]
+        return grad_in, (cat_grad, weight_grad, local_small, shared_small), order
+
+    def dots_of(grad_out, kept):
+        return jnp.sum(grad_out.astype(jnp.float32) * kept[4], axis=-1) / inner
 
     micros = range(micro_local)
     grads_flow = [cotangent_rows[micro] for micro in micros]
     flow = [input_rows[micro] for micro in micros]
     kept_all = []
     outputs = []
+    order = jnp.float32(0.0)
     for layer in range(section_count):
-        results = [forward(flow[micro], segment_rows[micro], layer) for micro in micros]
+        results = []
+        for micro in micros:
+            results.append(forward(flow[micro], segment_rows[micro], layer, order))
+            order = results[-1][2]
         flow = [pair[0] for pair in results]
         kept_all.append([pair[1] for pair in results])
         outputs.append(jnp.stack(flow))
@@ -333,10 +347,35 @@
         gathered_grads = [
             lax.all_gather(grads_flow[micro], "tensor", axis=0, tiled=True) for micro in micros
         ]
-        results = [
-            backward(grads_flow[micro], gathered_grads[micro], kept_all[layer][micro], layer)
-            for micro in micros
-        ]
+        if layer == section_count - 1:
+            own_dots = jnp.stack(
+                [dots_of(grads_flow[micro], kept_all[layer][micro]) for micro in micros]
+            )
+            dots_all = lax.all_gather(own_dots, "tensor", axis=1, tiled=True)
+            row_dots = [dots_all[micro][:, None] for micro in micros]
+        else:
+            row_dots = [
+                lax.all_gather(
+                    dots_of(grads_flow[micro], kept_all[layer][micro]),
+                    "tensor",
+                    axis=0,
+                    tiled=True,
+                )[:, None]
+                for micro in micros
+            ]
+        results = []
+        for micro in micros:
+            results.append(
+                backward(
+                    grads_flow[micro],
+                    gathered_grads[micro],
+                    row_dots[micro],
+                    kept_all[layer][micro],
+                    layer,
+                    order,
+                )
+            )
+            order = results[-1][2]
         grads_flow = [pair[0] for pair in results]
         in_grads[layer] = jnp.stack(grads_flow)
         summed = results[0][1]
@@ -344,6 +383,7 @@
             summed = jax.tree.map(jnp.add, summed, pair[1])
         cat_grad, weight_grad, local_small, shared_small = summed
         bc_first = 2 * inner_local
+        small_rows = -(-local_small.size // model_width)
         bc_sum = lax.psum_scatter(
             cat_grad[:, bc_first : bc_first + bc_width].T.astype(jnp.bfloat16),
             "tensor",
@@ -354,10 +394,20 @@
             cat_grad[:, :bc_first].astype(jnp.bfloat16),
             weight_grad.astype(jnp.bfloat16),
             jnp.concatenate(
-                [bc_sum, cat_grad[:, bc_first + bc_width :].T.astype(jnp.bfloat16)], axis=0
+                [
+                    bc_sum,
+                    cat_grad[:, bc_first + bc_width :].T.astype(jnp.bfloat16),
+                    jnp.pad(local_small, (0, small_rows * model_width - local_small.size))
+                    .reshape(small_rows, model_width)
+                    .astype(jnp.bfloat16),
+                ],
+                axis=0,
             ),
         )
-        totals[layer] = (lax.psum(big, ("pipe", "dp")), local_small, shared_small)
+        if layer < section_count - 1:
+            zero = 0.0 * totals[layer + 1][0][2][0, 0]
+            big = jax.tree.map(lambda value: value + zero, big)
+        totals[layer] = (lax.psum(big, ("pipe", "dp")), shared_small)
 
     def pick(values):
         chosen = values[0]
@@ -377,12 +427,12 @@
     layer_outputs = regroup(outputs)
     input_grads = regroup(in_grads)
     zx_total, out_total, rest_total = pick([total[0] for total in totals])
-    local_total = pick(lax.psum([total[1] for total in totals], ("pipe", "dp")))
-    shared_total = pick(lax.psum([total[2] for total in totals], ("pipe", "dp", "tensor")))
+    local_total = rest_total[bc_local + heads_local :].astype(jnp.float32).reshape(-1)
+    shared_total = pick(lax.psum([total[1] for total in totals], ("pipe", "dp", "tensor")))
     zx_total = zx_total.astype(jnp.float32)
     grad_zx = jnp.stack([zx_total[:, :inner_local], zx_total[:, inner_local:]])[None]
     grad_bc = rest_total[:bc_local].astype(jnp.float32).T[None]
-    grad_dt = rest_total[bc_local:].astype(jnp.float32).T[None]
+    grad_dt = rest_total[bc_local : bc_local + heads_local].astype(jnp.float32).T[None]
     pieces = []
     start = 0
     for size in (

time: 1120 us -> 1060 us (0.946)
  waiting for transfers between devices: 449 us -> 386 us
  other arithmetic: 132 us -> 149 us
    reduce_scatter x4, waiting for transfers between devices: 104 us -> 51.8 us  [forward(): lax.psum_scatter(partial.astype(jnp.bfloat16), 'tensor', scatter_dimensio...]
    all_gather x4, waiting for transfers between devices: 54.4 us -> 10.5 us  [local(): lax.all_gather(grads_flow[micro], 'tensor', axis=0, tiled=True)]
    all_gather x1, waiting for transfers between devices: 0.01 us -> 37.3 us  [local(): bc_all = lax.all_gather(bc_pack, ('pipe', 'tensor'), axis=0, tiled=True)]
    all_gather x5 -> x3, blocking collectives: 58.6 us -> 27.7 us  [the longest x2 19.2 us: local(): lax.all_gather(dots_of(grads_flow[micro], kept_all[layer][micro]), 'tenso...]
    all_gather x1 -> x2, waiting for transfers between devices: 39.1 us -> 10.8 us  [sections(): return lax.all_gather(value, 'pipe', axis=0)]
    reduce_scatter x2, waiting for transfers between devices: 0.02 us -> 27.1 us  [local(): lax.psum_scatter(cat_grad[:, bc_first:bc_first + bc_width].T.astype(jnp.b...]
    psum x2 -> x4, blocking collectives: 32.5 us -> 59.1 us  [forward(): squares = lax.psum(jnp.sum(gated * gated, axis=-1), 'tensor')]
    reduce_sum x4, other arithmetic: 14 us -> 28.9 us  [causal_conv(): result = result + kernel[offset] * earlier * same_doc[:, None]]
  transfers between devices with their start and end apart: 23 -> 25, of which waited for: 18 -> 16; matrix products, arithmetic and copies ran while one was open for 19% -> 38% of each run, Pallas kernels for 0% -> 0%
where the time goes in v2:
time: 1060 us; the launch traced here: 1050 us
  waiting for transfers between devices  386 us (36%)
  matrix products  195 us (18%)
  blocking collectives  152 us (14%)
  other arithmetic  149 us (14%)
  local copies, waits for them, and re-layouts  128 us (12%)
  between operations  29.7 us (3%)
    all_gather x4, waiting for transfers between devices, forward(): gathered = lax.all_gather(normed, 'tensor', axis=0, tiled=True)  98.6 us
    reduce_scatter x4, waiting for transfers between devices, backward(): lax.psum_scatter(spread_grad.astype(jnp.bfloat16), 'tensor', scatter_dime...  90.9 us
    psum x4, blocking collectives, forward(): squares = lax.psum(jnp.sum(gated * gated, axis=-1), 'tensor')  59.1 us
    psum x1, blocking collectives, local(): lax.psum([total[1] for total in totals], ('pipe', 'dp', 'tensor'))  55.5 us
    dot_general x12, matrix products, state_scan(): jnp.einsum('chts,cshp->cthp', affinity[:, None] * decays, weighted, preci...  52.5 us
    reduce_scatter x4, waiting for transfers between devices, forward(): lax.psum_scatter(partial.astype(jnp.bfloat16), 'tensor', scatter_dimensio...  51.8 us
    psum x2, waiting for transfers between devices, local(): totals[layer] = (lax.psum(big, ('pipe', 'dp')), shared_small)  45.3 us
    all_gather x1, waiting for transfers between devices, local(): bc_all = lax.all_gather(bc_pack, ('pipe', 'tensor'), axis=0, tiled=True)  37.3 us
  transfers between devices with their start and end apart: 25, of which 16 were waited for; matrix products, arithmetic and copies ran while one was open for 38% of the time, Pallas kernels for 0%

profile of v2, /device:TPU:0, one launch (start us, length us, event | category | flops | bytes accessed | tf_op | source)
XLA Modules:
  0.0 1049.4 jit_solution(11015564378456788350)
XLA Ops:
  13.1 9.8 all-reduce.112
  35.7 10.8 %all-gather.39.cloned.1.call-done = bf16[2,516,1024]{2,1,0:T(8,128)(2,1)} async-done(((bf16[1,516,1024]{2,1,0:T(8,128)(2,1)}), bf16[2,516,1024]{2,1,0:T(8,128)(2,1)}) %all-gather.39.cloned.1.call-update) | async-done | bytes 2113552 | tf_op jit(solution)/shard_map/all_gather | solution.py:146
  50.6 37.3 %all-gather.21.cloned.1.call-done = bf16[512,1152]{1,0:T(8,128)(2,1)} async-done(((bf16[32,1152]{1,0:T(8,128)(2,1)}), bf16[512,1152]{1,0:T(8,128)(2,1)}) %all-gather.21.cloned.1.call-update) | async-done | bytes 1179664 | tf_op jit(solution)/shard_map/all_gather | solution.py:172
  91.7 25.9 %all-gather.19.cloned.1.call-done = bf16[1024,1024]{1,0:T(8,128)(2,1)} async-done(((bf16[128,1024]{1,0:T(8,128)(2,1)}), bf16[1024,1024]{1,0:T(8,128)(2,1)}) %all-gather.19.cloned.1.call-update) | async-done | bytes 2097168 | tf_op jit(solution)/shard_map/all_gather | solution.py:225
  123.0 24.7 %all-gather.25.cloned.1.call-done = bf16[1024,1024]{1,0:T(8,128)(2,1)} async-done(((bf16[128,1024]{1,0:T(8,128)(2,1)}), bf16[1024,1024]{1,0:T(8,128)(2,1)}) %all-gather.25.cloned.1.call-update) | async-done | bytes 2097168 | tf_op jit(solution)/shard_map/all_gather | solution.py:225
  170.7 15.6 %psum.84 = f32[1024]{0:T(1024)S(1)} all-reduce(f32[1024]{0:T(1024)S(1)} %get-tuple-element.303), channel_id=1, replica_groups=mesh['pipe'=2,'dp'=2,'tensor'=8] {'tensor'}, use_global_device_ids=true, to_apply=%region_3.5 | all-reduce | flops 1024 | bytes 8192 | tf_op jit(solution)/shard_map/psum | solution.py:252
  195.8 6.8 fusion.201
  223.7 13.7 %psum.85 = f32[1024]{0:T(1024)S(1)} all-reduce(f32[1024]{0:T(1024)S(1)} %get-tuple-element.294), channel_id=1, replica_groups=mesh['pipe'=2,'dp'=2,'tensor'=8] {'tensor'}, use_global_device_ids=true, to_apply=%region_7.9 | all-reduce | flops 1024 | bytes 8192 | tf_op jit(solution)/shard_map/psum | solution.py:252
  241.4 25.3 %reduce-scatter.13.cloned.1.call-done = bf16[128,1024]{1,0:T(8,128)(2,1)} async-done(((bf16[1024,1024]{1,0:T(8,128)(2,1)}), bf16[128,1024]{1,0:T(8,128)(2,1)}) %reduce-scatter.13.cloned.1.call-update) | async-done | bytes 262160 | tf_op jit(solution)/shard_map/reduce_scatter | solution.py:256
  274.1 24.2 %all-gather.27.cloned.1.call-done = bf16[1024,1024]{1,0:T(8,128)(2,1)} async-done(((bf16[128,1024]{1,0:T(8,128)(2,1)}), bf16[1024,1024]{1,0:T(8,128)(2,1)}) %all-gather.27.cloned.1.call-update) | async-done | bytes 2097168 | tf_op jit(solution)/shard_map/all_gather | solution.py:225
  298.3 3.7 fusion.563
  304.7 23.8 %all-gather.29.cloned.1.call-done = bf16[1024,1024]{1,0:T(8,128)(2,1)} async-done(((bf16[128,1024]{1,0:T(8,128)(2,1)}), bf16[1024,1024]{1,0:T(8,128)(2,1)}) %all-gather.29.cloned.1.call-update) | async-done | bytes 2097168 | tf_op jit(solution)/shard_map/all_gather | solution.py:225
  361.2 15.5 %psum.86 = f32[1024]{0:T(1024)S(1)} all-reduce(f32[1024]{0:T(1024)} %get-tuple-element.277), channel_id=1, replica_groups=mesh['pipe'=2,'dp'=2,'tensor'=8] {'tensor'}, use_global_device_ids=true, to_apply=%region_11.13 | all-reduce | flops 1024 | bytes 8192 | tf_op jit(solution)/shard_map/psum | solution.py:252
  380.3 5.7 fusion.197
  404.6 3.6 fusion.620
  408.2 14.3 %psum.87 = f32[1024]{0:T(1024)} all-reduce(f32[1024]{0:T(1024)} %get-tuple-element.268), channel_id=1, replica_groups=mesh['pipe'=2,'dp'=2,'tensor'=8] {'tensor'}, use_global_device_ids=true, to_apply=%region_15.17 | all-reduce | flops 1024 | bytes 8192 | tf_op jit(solution)/shard_map/psum | solution.py:252
  424.4 26.5 %reduce-scatter.17.cloned.1.call-done = bf16[128,1024]{1,0:T(8,128)(2,1)} async-done(((bf16[1024,1024]{1,0:T(8,128)(2,1)}), bf16[128,1024]{1,0:T(8,128)(2,1)}) %reduce-scatter.17.cloned.1.call-update) | async-done | bytes 262160 | tf_op jit(solution)/shard_map/reduce_scatter | solution.py:256
  459.9 8.5 all_gather.62
  471.1 10.4 all-gather.35.cloned.1.call-done
  481.5 6.0 multiply_reduce_fusion.22
  506.7 7.0 fusion.25
  523.4 9.2 multiply_reduce_fusion.24
  538.5 3.7 fusion.621
  544.7 6.0 multiply_reduce_fusion.16
  569.8 5.7 fusion.27
  585.2 8.5 multiply_reduce_fusion.18
  600.1 5.0 fusion.622
  606.6 34.1 %reduce-scatter.23.cloned.1.call-done = bf16[128,1024]{1,0:T(8,128)(2,1)} async-done(((bf16[1024,1024]{1,0:T(8,128)(2,1)}), bf16[128,1024]{1,0:T(8,128)(2,1)}) %reduce-scatter.23.cloned.1.call-update) | async-done | bytes 262160 | tf_op jit(solution)/shard_map/reduce_scatter | solution.py:294
  654.9 3.8 fusion.350
  662.8 8.5 all-gather.5
  671.9 10.7 %all-gather.6 = f32[8,1,128]{2,1,0:T(1,128)S(1)} all-gather(f32[1,1,128]{2,1,0:T(1,128)S(1)} %multiply_bitcast_fusion), channel_id=1, replica_groups=mesh['pipe'=2,'dp'=2,'tensor'=8] {'tensor'}, dimensions={0}, use_global_device_ids=true | all-gather | bytes 4608 | tf_op jit(solution)/shard_map/all_gather | solution.py:358
  683.3 5.7 multiply_reduce_fusion.10
  690.7 6.9 fusion.29
  721.5 5.8 multiply_reduce_fusion.12
  730.9 3.8 fusion.623
  736.5 5.7 multiply_reduce_fusion.4
  744.0 7.0 fusion.31
  779.9 5.3 multiply_reduce_fusion.6
  795.6 3.7 convolution_convert_fusion
  810.2 8.7 all-reduce.118.cloned.1.call-done
  826.2 27.1 %reduce-scatter.29.cloned.1.call-done = bf16[32,1024]{1,0:T(8,128)(2,1)} async-done(((bf16[256,1024]{1,0:T(8,128)(2,1)}), bf16[32,1024]{1,0:T(8,128)(2,1)}) %reduce-scatter.29.cloned.1.call-update) | async-done | bytes 65552 | tf_op jit(solution)/shard_map/reduce_scatter | solution.py:387
  856.3 3.6 all-to-all-start
  860.2 10.1 all-to-all-done
  870.4 19.9 %reduce-scatter.21.cloned.1.call-done = bf16[128,1024]{1,0:T(8,128)(2,1)} async-done(((bf16[1024,1024]{1,0:T(8,128)(2,1)}), bf16[128,1024]{1,0:T(8,128)(2,1)}) %reduce-scatter.21.cloned.1.call-update) | async-done | bytes 262160 | tf_op jit(solution)/shard_map/reduce_scatter | solution.py:294
  890.3 36.9 %reduce-scatter.25.cloned.1.call-done = bf16[128,1024]{1,0:T(8,128)(2,1)} async-done(((bf16[1024,1024]{1,0:T(8,128)(2,1)}), bf16[128,1024]{1,0:T(8,128)(2,1)}) %reduce-scatter.25.cloned.1.call-update) | async-done | bytes 262160 | tf_op jit(solution)/shard_map/reduce_scatter | solution.py:294
  931.2 4.4 all-to-all-start.1
  935.6 55.5 %all-reduce.113 = (f32[2304]{0:T(1024)S(1)}, f32[2304]{0:T(1024)S(1)}) all-reduce(f32[2304]{0:T(1024)S(1)} %maximum_add_fusion.1, f32[2304]{0:T(1024)S(1)} %maximum_add_fusion.2), channel_id=1, replica_groups=mesh['pipe'=2,'dp'=2,'tensor'=8] {'pipe','dp','tensor'}, use_global_device_ids=true, to_apply=%region_81.83 | all-reduce | flops 4608 | bytes 36864 | tf_op jit(solution)/shard_map/psum | solution.py:431
  992.9 36.5 %all-reduce.120.cloned.1.call-done = (bf16[1024,512]{0,1:T(8,128)(2,1)}, bf16[1024,512]{0,1:T(8,128)(2,1)}, bf16[38,1024]{1,0:T(8,128)(2,1)}, bf16[256,1024]{1,0:T(8,128)(2,1)}, bf16[256,1024]{1,0:T(8,128)(2,1)}) async-done(((bf16[1024,512]{0,1:T(8,128)(2,1)}, bf16[1024,512]{0,1:T(8,128)(2,1)}, bf16[38,1024]{1,0:T(8,128)(2,1)}, bf16[256,1024]{1,0:T(8,128)(2,1)}, bf16[256,1024]{1,0:T(8,128)(2,1)}), ...) | async-done | bytes 3223568 | tf_op jit(solution)/shard_map/psum | solution.py:410
  (1438 shorter events, 358.7 us)
Async XLA Ops:
  7.2 39.3 %all-gather.39.cloned.1.call-start = ((), (), s32[]{:S(2)}) async-start(), calls=%async_computation.33 | async-start | bytes 3194880 | tf_op jit(solution)/shard_map/all_gather | solution.py:146
  10.2 77.7 %all-gather.21.cloned.1.call-start = ((), (), s32[]{:S(2)}) async-start(), calls=%async_computation.13 | async-start | bytes 1253376 | tf_op jit(solution)/shard_map/all_gather | solution.py:172
  11.3 106.3 %all-gather.19.cloned.1.call-start = ((), (), s32[]{:S(2)}) async-start(), calls=%async_computation.12 | async-start | bytes 2359296 | tf_op jit(solution)/shard_map/all_gather | solution.py:225
  24.9 122.8 %all-gather.25.cloned.1.call-start = ((), (), s32[]{:S(2)}) async-start(), calls=%async_computation.16 | async-start | bytes 2359296 | tf_op jit(solution)/shard_map/all_gather | solution.py:225
  25.4 164.0 %all-gather.23.cloned.1.call-start = ((), (), s32[]{:S(2)}) async-start(), calls=%async_computation.14 | async-start | bytes 1572864 | tf_op jit(solution)/shard_map/all_gather | solution.py:146
  26.0 215.3 %reduce-scatter.11.cloned.1.call-start = ((), (), s32[]{:S(2)}) async-start(), calls=%async_computation.15 | async-start | bytes 2359296 | tf_op jit(solution)/shard_map/reduce_scatter | solution.py:256
  26.8 124.5 %copy-start.382 = (f32[4]{0:T(128)}, f32[4]{0:T(128)S(1)}, u32[]{:S(2)}) copy-start(f32[4]{0:T(128)S(1)} %get-tuple-element.426) | copy-start | bytes 52
  26.8 124.5 %copy-start.384 = (f32[4]{0:T(128)}, f32[4]{0:T(128)S(1)}, u32[]{:S(2)}) copy-start(f32[4]{0:T(128)S(1)} %get-tuple-element.427) | copy-start | bytes 52
  27.4 125.9 %copy-start.311 = (f32[1,256]{1,0:T(1,128)}, f32[1,256]{1,0:T(1,128)S(1)}, u32[]{:S(2)}) copy-start(f32[1,256]{1,0:T(1,128)S(1)} %get-tuple-element.417) | copy-start | bytes 3076
  27.4 125.9 %copy-start.313 = (f32[1,256]{1,0:T(1,128)}, f32[1,256]{1,0:T(1,128)S(1)}, u32[]{:S(2)}) copy-start(f32[1,256]{1,0:T(1,128)S(1)} %get-tuple-element.418) | copy-start | bytes 3076
  27.4 125.9 %copy-start.315 = (f32[1,256]{1,0:T(1,128)}, f32[1,256]{1,0:T(1,128)S(1)}, u32[]{:S(2)}) copy-start(f32[1,256]{1,0:T(1,128)S(1)} %get-tuple-element.419) | copy-start | bytes 3076
  27.4 125.9 %copy-start.317 = (f32[1,256]{1,0:T(1,128)}, f32[1,256]{1,0:T(1,128)S(1)}, u32[]{:S(2)}) copy-start(f32[1,256]{1,0:T(1,128)S(1)} %get-tuple-element.420) | copy-start | bytes 3076
  27.4 125.9 %copy-start.320 = (f32[1,256]{1,0:T(1,128)}, f32[1,256]{1,0:T(1,128)S(1)}, u32[]{:S(2)}) copy-start(f32[1,256]{1,0:T(1,128)S(1)} %get-tuple-element.421) | copy-start | bytes 3076
  31.9 121.4 %copy-start.192 = (f32[1024]{0:T(1024)}, f32[1024]{0:T(1024)S(1)}, u32[]{:S(2)}) copy-start(f32[1024]{0:T(1024)S(1)} %get-tuple-element.518) | copy-start | bytes 12292
  31.9 121.4 %copy-start.196 = (f32[1024]{0:T(1024)}, f32[1024]{0:T(1024)S(1)}, u32[]{:S(2)}) copy-start(f32[1024]{0:T(1024)S(1)} %get-tuple-element.519) | copy-start | bytes 12292
  31.9 121.4 %copy-start.200 = (f32[1024]{0:T(1024)}, f32[1024]{0:T(1024)S(1)}, u32[]{:S(2)}) copy-start(f32[1024]{0:T(1024)S(1)} %get-tuple-element.520) | copy-start | bytes 12292
  33.9 127.5 %copy-start.235 = (f32[4,256]{1,0:T(4,128)}, f32[4,256]{1,0:T(4,128)S(1)}, u32[]{:S(2)}) copy-start(f32[4,256]{1,0:T(4,128)S(1)} %get-tuple-element.513) | copy-start | bytes 12292
  33.9 127.5 %copy-start.282 = (f32[4,256]{1,0:T(4,128)}, f32[4,256]{1,0:T(4,128)S(1)}, u32[]{:S(2)}) copy-start(f32[4,256]{1,0:T(4,128)S(1)} %get-tuple-element.512) | copy-start | bytes 12292
  34.5 125.4 %copy-start.307 = (f32[4]{0:T(128)}, f32[4]{0:T(128)S(1)}, u32[]{:S(2)}) copy-start(f32[4]{0:T(128)S(1)} %get-tuple-element.572) | copy-start | bytes 52
  47.9 99.8 %copy-start.398 = (bf16[4,1024]{1,0:T(4,128)(2,1)}, bf16[4,1024]{1,0:T(4,128)(2,1)S(1)}, u32[]{:S(2)}) copy-start(bf16[4,1024]{1,0:T(4,128)(2,1)S(1)} %get-tuple-element.335) | copy-start | bytes 24580
  50.5 97.2 %copy-start.138 = (bf16[512,1024]{1,0:T(8,128)(2,1)}, bf16[512,1024]{1,0:T(8,128)(2,1)S(1)}, u32[]{:S(2)}) copy-start(bf16[512,1024]{1,0:T(8,128)(2,1)S(1)} %get-tuple-element.333) | copy-start | bytes 3145732
  195.6 71.0 %reduce-scatter.13.cloned.1.call-start = ((), (), s32[]{:S(2)}) async-start(), calls=%async_computation.17 | async-start | bytes 2359296 | tf_op jit(solution)/shard_map/reduce_scatter | solution.py:256
  223.6 74.7 %copy-start.171 = (bf16[256,1024]{1,0:T(8,128)(2,1)S(1)}, bf16[256,1024]{1,0:T(8,128)(2,1)}, u32[]{:S(2)}) copy-start(bf16[256,1024]{1,0:T(8,128)(2,1)} %get-tuple-element.342) | copy-start | bytes 1572868
  223.6 74.7 %copy-start.400 = (bf16[4,1024]{1,0:T(4,128)(2,1)S(1)}, bf16[4,1024]{1,0:T(4,128)(2,1)}, u32[]{:S(2)}) copy-start(bf16[4,1024]{1,0:T(4,128)(2,1)} %get-tuple-element.334) | copy-start | bytes 24580
  223.6 74.7 %all-gather.27.cloned.1.call-start = ((), (), s32[]{:S(2)}) async-start(), calls=%async_computation.18 | async-start | bytes 2359296 | tf_op jit(solution)/shard_map/all_gather | solution.py:225
  270.2 58.3 %all-gather.29.cloned.1.call-start = ((), (), s32[]{:S(2)}) async-start(), calls=%async_computation.20 | async-start | bytes 2359296 | tf_op jit(solution)/shard_map/all_gather | solution.py:225
  271.0 153.4 %reduce-scatter.15.cloned.1.call-start = ((), (), s32[]{:S(2)}) async-start(), calls=%async_computation.19 | async-start | bytes 2359296 | tf_op jit(solution)/shard_map/reduce_scatter | solution.py:256
  379.9 71.0 %reduce-scatter.17.cloned.1.call-start = ((), (), s32[]{:S(2)}) async-start(), calls=%async_computation.21 | async-start | bytes 2359296 | tf_op jit(solution)/shard_map/reduce_scatter | solution.py:256
  408.2 73.4 %copy-start.12 = (f32[1024,256]{0,1:T(8,128)S(1)}, f32[1024,256]{0,1:T(8,128)}, u32[]{:S(2)}) copy-start(f32[1024,256]{0,1:T(8,128)} %copy-done.11) | copy-start | bytes 3145732
  408.2 73.3 %all-gather.35.cloned.1.call-start = ((), (), s32[]{:S(2)}) async-start(), calls=%async_computation.31 | async-start | bytes 2359296 | tf_op jit(solution)/shard_map/all_gather | solution.py:348
  453.7 91.0 %all-gather.37.cloned.1.call-start = ((), (), s32[]{:S(2)}) async-start(), calls=%async_computation.32 | async-start | bytes 2359296 | tf_op jit(solution)/shard_map/all_gather | solution.py:348
  471.0 135.6 %reduce-scatter.19.cloned.1.call-start = ((), (), s32[]{:S(2)}) async-start(), calls=%async_computation.22 | async-start | bytes 2359296 | tf_op jit(solution)/shard_map/reduce_scatter | solution.py:294
  544.6 96.1 %reduce-scatter.23.cloned.1.call-start = ((), (), s32[]{:S(2)}) async-start(), calls=%async_computation.25 | async-start | bytes 2359296 | tf_op jit(solution)/shard_map/reduce_scatter | solution.py:294
  605.2 78.1 %all-gather.31.cloned.1.call-start = ((), (), s32[]{:S(2)}) async-start(), calls=%async_computation.23 | async-start | bytes 2359296 | tf_op jit(solution)/shard_map/all_gather | solution.py:348
  645.8 90.6 %all-gather.33.cloned.1.call-start = ((), (), s32[]{:S(2)}) async-start(), calls=%async_computation.26 | async-start | bytes 2359296 | tf_op jit(solution)/shard_map/all_gather | solution.py:348
  646.4 131.8 %reduce-scatter.27.cloned.1.call-start = ((), (), s32[]{:S(2)}) async-start(), calls=%async_computation.28 | async-start | bytes 589824 | tf_op jit(solution)/shard_map/reduce_scatter | solution.py:387
  662.8 156.1 %all-reduce.118.cloned.1.call-start = ((), (), s32[]{:S(2)}) async-start(), calls=%async_computation.29 | async-start | bytes 163840 | tf_op jit(solution)/shard_map/psum | solution.py:410
  779.7 73.6 %reduce-scatter.29.cloned.1.call-start = ((), (), s32[]{:S(2)}) async-start(), calls=%async_computation.30 | async-start | bytes 589824 | tf_op jit(solution)/shard_map/reduce_scatter | solution.py:387
  794.8 95.5 %reduce-scatter.21.cloned.1.call-start = ((), (), s32[]{:S(2)}) async-start(), calls=%async_computation.24 | async-start | bytes 2359296 | tf_op jit(solution)/shard_map/reduce_scatter | solution.py:294
  795.5 131.6 %reduce-scatter.25.cloned.1.call-start = ((), (), s32[]{:S(2)}) async-start(), calls=%async_computation.27 | async-start | bytes 2359296 | tf_op jit(solution)/shard_map/reduce_scatter | solution.py:294
  799.3 230.1 %all-reduce.120.cloned.1.call-start = ((), (), s32[]{:S(2)}) async-start(), calls=%async_computation.34 | async-start | bytes 6455296 | tf_op jit(solution)/shard_map/psum | solution.py:410
  855.1 72.0 %copy-start.39 = (bf16[4,1,128,1024]{3,2,1,0:T(8,128)(2,1)S(1)}, bf16[4,1,128,1024]{3,2,1,0:T(8,128)(2,1)}, u32[]{:S(2)}) copy-start(bf16[4,1,128,1024]{3,2,1,0:T(8,128)(2,1)} %param.17) | copy-start | bytes 3145732
  855.1 72.0 %copy-start.248 = (f32[1,1024]{1,0:T(1,128)S(1)}, f32[1,1024]{1,0:T(1,128)}, u32[]{:S(2)}) copy-start(f32[1,1024]{1,0:T(1,128)} %copy-done.247) | copy-start | bytes 12292
  855.2 73.3 %copy-start.465 = (f32[128]{0:T(128)S(1)}, f32[128]{0:T(128)}, u32[]{:S(2)}) copy-start(f32[128]{0:T(128)} %get-tuple-element.542) | copy-start | bytes 1540
  855.2 73.3 %copy-start.466 = (f32[128]{0:T(128)S(1)}, f32[128]{0:T(128)}, u32[]{:S(2)}) copy-start(f32[128]{0:T(128)} %get-tuple-element.575) | copy-start | bytes 1540
  856.3 13.9 %all-to-all-start = ((bf16[2,2,128,1024]{3,2,1,0:T(8,128)(2,1)}), bf16[2,2,128,1024]{3,2,1,0:T(8,128)(2,1)S(1)}, u32[]{:S(2)}, u32[]{:S(2)}) async-start(bf16[2,2,128,1024]{3,2,1,0:T(8,128)(2,1)} %pad_maximum_fusion.6), calls=%async_computation.4 | async-start | bytes 2097152 | tf_op jit(solution)/shard_map/all_to_all | solution.py:424
  930.0 99.4 %copy-start.240 = (bf16[38,1024]{1,0:T(8,128)(2,1)S(1)}, bf16[38,1024]{1,0:T(8,128)(2,1)}, u32[]{:S(2)}) copy-start(bf16[38,1024]{1,0:T(8,128)(2,1)} %all-reduce.118.cloned.1.call-done) | copy-start | bytes 233476
  931.2 107.9 %all-to-all-start.1 = ((bf16[2,2,128,1024]{3,2,1,0:T(8,128)(2,1)}), bf16[2,2,128,1024]{3,2,1,0:T(8,128)(2,1)}, u32[]{:S(2)}, u32[]{:S(2)}) async-start(bf16[2,2,128,1024]{3,2,1,0:T(8,128)(2,1)} %pad_maximum_fusion.7), calls=%async_computation.9 | async-start | bytes 2097152 | tf_op jit(solution)/shard_map/all_to_all | solution.py:424
  (470 other events, 3753.6 us)
Sparse Core Ops, SparseCore 0:
  10.3 36.1 all-gather.38
  49.4 38.3 all-gather.20
  89.4 28.1 all-gather.18
  119.1 28.5 all-gather.24
  149.1 20.7 all-gather.22
  195.7 33.8 reduce-scatter.10
  232.0 34.6 reduce-scatter.12
  270.4 27.8 all-gather.26
  299.9 28.5 all-gather.28
  380.1 33.8 reduce-scatter.14
  416.3 34.6 reduce-scatter.16
  453.8 27.6 all-gather.34
  483.1 28.5 all-gather.36
  544.8 35.2 reduce-scatter.18
  605.3 35.3 reduce-scatter.22
  646.0 27.7 all-gather.30
  675.2 28.6 all-gather.32
  706.0 30.4 reduce-scatter.26
  779.9 39.0 all-reduce.117
  821.6 31.7 reduce-scatter.28
  856.3 33.9 reduce-scatter.20
  892.7 34.4 reduce-scatter.24
  931.9 97.5 all-reduce.119
